TPU v7x, 128 devices: a whole 4x4x4 slice. The times are simulated.
128 devices in a mesh: rep: 32 (over z, y, core), head: 4 (over x).
Axes of the slice: x: 4, y: 4, z: 4, core: 2. Of those that a mesh axis runs over, the one named last changes fastest.
Arguments:
- query_latent: bfloat16 [4, 160, 1536], P(None, 'rep'), may hold values from -48 to 48
- new_entry: bfloat16 [4, 160, 576], P(None, 'rep'), may hold values from -6 to 6
- cache_latent: bfloat16 [10240, 64, 512], P('rep'), may hold values from -6 to 6
- cache_rope: bfloat16 [10240, 4096], P('rep'), may hold values from -6 to 6
- block_table: int32 [160, 64], P('rep'), may hold values from 0 to 319, as said below
- context_len: int32 [160], P('rep'), may hold values from 512 to 4092, as said below
- owner_rows: int32 [32], replicated, may hold values from 0 to 31, each once
- query_up: bfloat16 [1536, 12288], P(('rep', 'head')), may hold values from -0.15625 to 0.15625
- key_up: bfloat16 [512, 8192], P(('rep', 'head')), may hold values from -0.75 to 0.75
- value_up: bfloat16 [512, 8192], P(('rep', 'head')), may hold values from -1 to 1
Outputs:
- attention_out: bfloat16 [4, 160, 8192], P(None, 'rep', 'head')
Inputs may be any that keep to these rules, and one draw needn't show every extreme that they name: `block_table`: within each replica the block tables of its 5 requests name every page of its pool once. `context_len`: every replica has a request of length 4092. `owner_rows`: A permutation.
All inputs are finite; a program needn't handle non-finite values.
Results may differ from a plain program's by a relative error of at most 0.035.
Values may be sent and summed in bfloat16 or wider, within the bound.
A program may use at most 192 MiB of HBM per device.

v0:
```python
import jax
import jax.numpy as jnp
from jax import lax
from jax.sharding import PartitionSpec as P

LAT = 512
DN = 128
DR = 64


def rotate_pairs(values, positions):
    half_width = values.shape[-1] // 2
    frequency = 10000.0 ** (-jnp.arange(half_width, dtype=jnp.float32) / half_width)
    angles = positions[..., None].astype(jnp.float32) * frequency
    lower_half = values[..., :half_width]
    upper_half = values[..., half_width:]
    cosine = jnp.cos(angles)
    sine = jnp.sin(angles)
    return jnp.concatenate(
        [lower_half * cosine - upper_half * sine, upper_half * cosine + lower_half * sine], axis=-1
    )


def attend_request(query_lat, query_rot, latent, rotary, new_lat, new_rot, length):
    score_scale = (DN + DR) ** (-0.5)
    cached_scores = jnp.einsum("shl,tl->sht", query_lat, latent, preferred_element_type=jnp.float32)
    cached_scores = cached_scores + jnp.einsum(
        "shc,tc->sht", query_rot, rotary, preferred_element_type=jnp.float32
    )
    cached_scores = cached_scores * score_scale
    token_index = jnp.arange(latent.shape[0], dtype=jnp.int32)
    cached_scores = jnp.where(token_index[None, None, :] < length, cached_scores, -1e30)
    fresh_scores = jnp.einsum("shl,ul->shu", query_lat, new_lat, preferred_element_type=jnp.float32)
    fresh_scores = fresh_scores + jnp.einsum(
        "shc,uc->shu", query_rot, new_rot, preferred_element_type=jnp.float32
    )
    fresh_scores = fresh_scores * score_scale
    step_index = jnp.arange(new_lat.shape[0], dtype=jnp.int32)
    fresh_scores = jnp.where(
        step_index[None, None, :] <= step_index[:, None, None], fresh_scores, -1e30
    )
    scores = jnp.concatenate([cached_scores, fresh_scores], axis=2)
    weights = jax.nn.softmax(scores, axis=2).astype(jnp.bfloat16)
    cached_count = latent.shape[0]
    mixed_latent = jnp.einsum(
        "sht,tl->shl", weights[:, :, :cached_count], latent, preferred_element_type=jnp.float32
    )
    mixed_latent = mixed_latent + jnp.einsum(
        "shu,ul->shl", weights[:, :, cached_count:], new_lat, preferred_element_type=jnp.float32
    )
    return mixed_latent.astype(jnp.bfloat16)


def on_device(
    query_latent,
    new_entry,
    cache_latent,
    cache_rope,
    block_table,
    context_len,
    owner_rows,
    query_up,
    key_up,
    value_up,
):
    highest = lax.Precision.HIGHEST
    part_query, part_key, part_value = (
        lax.all_to_all(query_up, "head", split_axis=1, concat_axis=0, tiled=True),
        lax.all_to_all(key_up, "head", split_axis=1, concat_axis=0, tiled=True),
        lax.all_to_all(value_up, "head", split_axis=1, concat_axis=0, tiled=True),
    )
    key_local, value_local = (
        lax.all_gather(part_key, "rep", axis=0, tiled=True),
        lax.all_gather(part_value, "rep", axis=0, tiled=True),
    )
    head_count = key_local.shape[1] // DN
    key_heads = key_local.reshape(LAT, head_count, DN)
    step_count, request_count, query_rank = query_latent.shape
    owners = owner_rows.shape[0]
    ordered = jnp.take(
        query_latent.reshape(step_count, request_count, owners, query_rank // owners),
        owner_rows,
        axis=2,
    )
    ordered = ordered.reshape(step_count * request_count, query_rank)
    ordered_wide = ordered.astype(jnp.float32)
    shard_rows = lax.all_gather(part_query, "rep", axis=0, tiled=True)
    row_count = shard_rows.shape[0]
    divided = shard_rows.reshape(row_count, head_count, DN + DR)
    absorbed = jnp.einsum(
        "nhd,lhd->nhl", divided[:, :, :DN], key_heads, preferred_element_type=jnp.float32
    )
    lat_total = jnp.einsum("rn,nhl->rhl", ordered_wide, absorbed, precision=highest)
    rot_total = jnp.einsum(
        "rn,nhc->rhc", ordered, divided[:, :, DN:], preferred_element_type=jnp.float32
    )
    lat_total, rot_total = (lat_total, rot_total)
    query_lat = lat_total.astype(jnp.bfloat16).reshape(step_count, request_count, head_count, LAT)
    query_raw = rot_total.reshape(step_count, request_count, head_count, DR)
    positions = context_len[None, :] + jnp.arange(step_count, dtype=jnp.int32)[:, None]
    query_rot = rotate_pairs(query_raw, positions[:, :, None]).astype(jnp.bfloat16)
    new_lat = new_entry[:, :, :LAT]
    new_rot = rotate_pairs(new_entry[:, :, LAT:].astype(jnp.float32), positions).astype(
        jnp.bfloat16
    )
    slot_count = block_table.shape[1] * cache_latent.shape[1]

    def one_request(request_items):
        page_ids, length, one_lat, one_rot, fresh_lat, fresh_rot = request_items
        latent = cache_latent[page_ids].reshape(slot_count, LAT)
        rotary = cache_rope[page_ids].reshape(slot_count, DR)
        return attend_request(one_lat, one_rot, latent, rotary, fresh_lat, fresh_rot, length)

    attended = lax.map(
        one_request,
        (
            block_table,
            context_len,
            jnp.swapaxes(query_lat, 0, 1),
            jnp.swapaxes(query_rot, 0, 1),
            jnp.swapaxes(new_lat, 0, 1),
            jnp.swapaxes(new_rot, 0, 1),
        ),
    )
    value_heads = value_local.reshape(LAT, head_count, DN)
    result = jnp.einsum("ishl,lhd->sihd", attended, value_heads, preferred_element_type=jnp.float32)
    return result.reshape(step_count, request_count, head_count * DN).astype(jnp.bfloat16)


def solution(mesh):
    return jax.shard_map(
        on_device,
        mesh=mesh,
        in_specs=(
            P(None, "rep", None),
            P(None, "rep", None),
            P("rep", None, None),
            P("rep", None),
            P("rep", None),
            P("rep"),
            P(),
            P(("rep", "head"), None),
            P(("rep", "head"), None),
            P(("rep", "head"), None),
        ),
        out_specs=P(None, "rep", "head"),
        check_vma=False,
    )
```

profile of v0, /device:TPU:1, one launch (start us, length us, event | category | flops | bytes accessed | tf_op | source)
XLA Modules:
  0.0 374.1 jit_solution(2771856903413983241)
XLA Ops:
  6.6 9.5 %all_to_all.57 = bf16[4,4,2048]{2,0,1:T(4,128)(2,1)S(1)} all-to-all(bf16[4,4,2048]{2,0,1:T(4,128)(2,1)} %bitcast.144), channel_id=1, replica_groups=mesh['rep'=32,'head'=4] {'head'}, dimensions={1} | all-to-all | bytes 131072 | tf_op jit(solution)/shard_map/all_to_all | solution.py:69
  16.8 7.7 %all_to_all.58 = bf16[4,4,2048]{2,0,1:T(4,128)(2,1)S(1)} all-to-all(bf16[4,4,2048]{2,0,1:T(4,128)(2,1)} %bitcast.145), channel_id=1, replica_groups=mesh['rep'=32,'head'=4] {'head'}, dimensions={1} | all-to-all | bytes 131072 | tf_op jit(solution)/shard_map/all_to_all | solution.py:70
  25.2 1.2 all_to_all.46
  26.6 8.6 %all_to_all.59 = bf16[12,4,3072]{2,0,1:T(8,128)(2,1)S(1)} all-to-all(bf16[12,4,3072]{2,0,1:T(8,128)(2,1)S(1)} %copy.72), channel_id=1, replica_groups=mesh['rep'=32,'head'=4] {'head'}, dimensions={1} | all-to-all | bytes 589824 | tf_op jit(solution)/shard_map/all_to_all | solution.py:68
  39.4 23.8 %all-gather.4.cloned.1.call-done = bf16[512,2048]{1,0:T(8,128)(2,1)} async-done(((bf16[16,2048]{1,0:T(8,128)(2,1)}), bf16[512,2048]{1,0:T(8,128)(2,1)}) %all-gather.4.cloned.1.call-update) | async-done | bytes 2097168 | tf_op jit(solution)/shard_map/all_gather | solution.py:73
  63.3 2.9 copy.71
  66.1 42.7 %all-gather.8.cloned.1.call-done = bf16[512,2048]{1,0:T(8,128)(2,1)} async-done(((bf16[16,2048]{1,0:T(8,128)(2,1)}), bf16[512,2048]{1,0:T(8,128)(2,1)}) %all-gather.8.cloned.1.call-update) | async-done | bytes 2097168 | tf_op jit(solution)/shard_map/all_gather | solution.py:74
  108.8 3.9 %copy.85 = bf16[512,2048]{0,1:T(8,128)(2,1)} copy(bf16[512,2048]{1,0:T(8,128)(2,1)} %all-gather.8.cloned.1.call-done) | data formatting | bytes 4194304 | tf_op jit(solution)/shard_map/all_gather | solution.py:74
  112.7 53.1 %all-gather.6.cloned.1.call-done = bf16[1536,3072]{1,0:T(8,128)(2,1)} async-done(((bf16[48,3072]{1,0:T(8,128)(2,1)}), bf16[1536,3072]{1,0:T(8,128)(2,1)}) %all-gather.6.cloned.1.call-update) | async-done | bytes 9437200 | tf_op jit(solution)/shard_map/all_gather | solution.py:87
  165.8 12.7 %copy.73 = bf16[1536,3072]{0,1:T(8,128)(2,1)} copy(bf16[1536,3072]{1,0:T(8,128)(2,1)} %all-gather.6.cloned.1.call-done) | data formatting | bytes 18874368 | tf_op jit(solution)/shard_map/all_gather | solution.py:87
  178.5 3.3 fusion.40
  182.1 20.6 %fusion.38 = f32[16,512,1536]{2,1,0:T(8,128)} fusion(bf16[512,16,128]{0,2,1:T(8,128)(2,1)S(1)} %bitcast.136, bf16[1536,16,192]{0,2,1:T(8,128)(2,1)} %bitcast.135), kind=kOutput, calls=%fused_computation.51 | convolution fusion | flops 3221225472 | bytes 58720256 | tf_op jit(solution)/shard_map/nhd,lhd->nhl/dot_general | solution.py:90
  202.8 27.5 %fusion.41 = bf16[20,16,512]{2,0,1:T(8,128)(2,1)S(1)} fusion(f32[16,512,1536]{2,1,0:T(8,128)} %fusion.38, bf16[20,1536]{1,0:T(8,128)(2,1)S(1)} %gather.15, pred[1536]{0:T(1024)(128)(4,1)S(1)} %broadcast_in_dim.65), kind=kOutput, calls=%fused_computation.55 | convolution fusion | flops 3020093440 | bytes 50722304 | tf_op jit(solution)/shard_map/rn,nhl->rhl/dot_general | solution.py:93
  230.3 134.1 %while.10 = (s32[]{:T(128)}, bf16[5,4,16,512]{3,2,1,0:T(8,128)(2,1)}, s32[5]{0:T(128)}, bf16[5,4,16,512]{3,2,0,1:T(8,128)(2,1)S(1)}, s32[5,64]{1,0:T(8,128)}, /*...) while((s32[]{:T(128)}, ...), condition=%wide.region_4.5_spmd, body=%wide.region_0.4_spmd.sunk | while | flops 573939584 | bytes 43057872 | solution.py:114
  231.2 9.7 %gather_fusion = bf16[64,64,512]{2,1,0:T(8,128)(2,1)} fusion(bf16[320,64,512]{2,1,0:T(8,128)(2,1)} %get-tuple-element.224, s32[1024]{0:T(1024)S(1)} %pad_clamp_fusion.3), kind=kCustom, calls=%fused_computation.clone.1 | custom fusion | bytes 8388864 | tf_op jit(solution)/shard_map/while/body/eval_jaxpr/gather | solution.py:110
  241.0 4.5 %fusion.85 = f32[4,16,4096]{2,1,0:T(8,128)} fusion(bf16[4096,512,1]{1,0,2:T(8,128)(2,1)} %bitcast.132, bf16[5,4,16,512]{3,2,0,1:T(8,128)(2,1)S(1)} %get-tuple-element.222, s32[]{:T(128)} %get-tuple-element.208), kind=kOutput, calls=%fused_computation.21.clone.1 | convolution fusion | flops 268435456 | bytes 5308420 | tf_op jit(solution)/shard_map/while/body/eval_jaxpr/shl,tl->sht/dot_general | solution.py:26
  245.5 1.0 gather_fusion.1
  246.5 2.1 reshape.208
  248.6 1.4 dynamic_slice.82
  250.7 2.1 fusion.86
  255.9 1.5 fusion.89
  258.1 9.7 %gather_fusion = bf16[64,64,512]{2,1,0:T(8,128)(2,1)} fusion(bf16[320,64,512]{2,1,0:T(8,128)(2,1)} %get-tuple-element.224, s32[1024]{0:T(1024)S(1)} %pad_clamp_fusion.3), kind=kCustom, calls=%fused_computation.clone.1 | custom fusion | bytes 8388864 | tf_op jit(solution)/shard_map/while/body/eval_jaxpr/gather | solution.py:110
  267.8 4.5 %fusion.85 = f32[4,16,4096]{2,1,0:T(8,128)} fusion(bf16[4096,512,1]{1,0,2:T(8,128)(2,1)} %bitcast.132, bf16[5,4,16,512]{3,2,0,1:T(8,128)(2,1)S(1)} %get-tuple-element.222, s32[]{:T(128)} %get-tuple-element.208), kind=kOutput, calls=%fused_computation.21.clone.1 | convolution fusion | flops 268435456 | bytes 5308420 | tf_op jit(solution)/shard_map/while/body/eval_jaxpr/shl,tl->sht/dot_general | solution.py:26
  272.3 1.0 gather_fusion.1
  273.3 2.1 reshape.208
  275.4 1.4 dynamic_slice.82
  277.5 2.1 fusion.86
  282.7 1.5 fusion.89
  284.8 9.7 %gather_fusion = bf16[64,64,512]{2,1,0:T(8,128)(2,1)} fusion(bf16[320,64,512]{2,1,0:T(8,128)(2,1)} %get-tuple-element.224, s32[1024]{0:T(1024)S(1)} %pad_clamp_fusion.3), kind=kCustom, calls=%fused_computation.clone.1 | custom fusion | bytes 8388864 | tf_op jit(solution)/shard_map/while/body/eval_jaxpr/gather | solution.py:110
  294.6 4.5 %fusion.85 = f32[4,16,4096]{2,1,0:T(8,128)} fusion(bf16[4096,512,1]{1,0,2:T(8,128)(2,1)} %bitcast.132, bf16[5,4,16,512]{3,2,0,1:T(8,128)(2,1)S(1)} %get-tuple-element.222, s32[]{:T(128)} %get-tuple-element.208), kind=kOutput, calls=%fused_computation.21.clone.1 | convolution fusion | flops 268435456 | bytes 5308420 | tf_op jit(solution)/shard_map/while/body/eval_jaxpr/shl,tl->sht/dot_general | solution.py:26
  299.1 1.0 gather_fusion.1
  300.1 2.1 reshape.208
  302.2 1.4 dynamic_slice.82
  304.2 2.1 fusion.86
  309.4 1.5 fusion.89
  311.6 9.7 %gather_fusion = bf16[64,64,512]{2,1,0:T(8,128)(2,1)} fusion(bf16[320,64,512]{2,1,0:T(8,128)(2,1)} %get-tuple-element.224, s32[1024]{0:T(1024)S(1)} %pad_clamp_fusion.3), kind=kCustom, calls=%fused_computation.clone.1 | custom fusion | bytes 8388864 | tf_op jit(solution)/shard_map/while/body/eval_jaxpr/gather | solution.py:110
  321.3 4.5 %fusion.85 = f32[4,16,4096]{2,1,0:T(8,128)} fusion(bf16[4096,512,1]{1,0,2:T(8,128)(2,1)} %bitcast.132, bf16[5,4,16,512]{3,2,0,1:T(8,128)(2,1)S(1)} %get-tuple-element.222, s32[]{:T(128)} %get-tuple-element.208), kind=kOutput, calls=%fused_computation.21.clone.1 | convolution fusion | flops 268435456 | bytes 5308420 | tf_op jit(solution)/shard_map/while/body/eval_jaxpr/shl,tl->sht/dot_general | solution.py:26
  326.8 2.1 reshape.208
  328.9 1.4 dynamic_slice.82
  331.0 2.1 fusion.86
  336.2 1.5 fusion.89
  338.4 9.7 %gather_fusion = bf16[64,64,512]{2,1,0:T(8,128)(2,1)} fusion(bf16[320,64,512]{2,1,0:T(8,128)(2,1)} %get-tuple-element.224, s32[1024]{0:T(1024)S(1)} %pad_clamp_fusion.3), kind=kCustom, calls=%fused_computation.clone.1 | custom fusion | bytes 8388864 | tf_op jit(solution)/shard_map/while/body/eval_jaxpr/gather | solution.py:110
  348.1 4.5 %fusion.85 = f32[4,16,4096]{2,1,0:T(8,128)} fusion(bf16[4096,512,1]{1,0,2:T(8,128)(2,1)} %bitcast.132, bf16[5,4,16,512]{3,2,0,1:T(8,128)(2,1)S(1)} %get-tuple-element.222, s32[]{:T(128)} %get-tuple-element.208), kind=kOutput, calls=%fused_computation.21.clone.1 | convolution fusion | flops 268435456 | bytes 5308420 | tf_op jit(solution)/shard_map/while/body/eval_jaxpr/shl,tl->sht/dot_general | solution.py:26
  353.7 2.1 reshape.208
  355.8 1.4 dynamic_slice.82
  357.8 2.1 fusion.86
  363.0 1.5 fusion.89
  364.5 2.4 fusion.44
  (120 shorter events, 30.8 us)
Async XLA Ops:
  6.5 29.5 %copy-start.3 = (bf16[4,5,1536]{2,0,1:T(4,128)(2,1)S(1)}, bf16[4,5,1536]{2,0,1:T(4,128)(2,1)}, u32[]{:S(2)}) copy-start(bf16[4,5,1536]{2,0,1:T(4,128)(2,1)} %param.12) | copy-start | bytes 184324
  6.5 29.8 %copy-start.6 = (s32[32]{0:T(128)S(1)}, s32[32]{0:T(128)}, u32[]{:S(2)}) copy-start(s32[32]{0:T(128)} %param.18) | copy-start | bytes 388
  6.5 31.1 %copy-start.5 = (s32[5]{0:T(128)S(1)}, s32[5]{0:T(128)}, u32[]{:S(2)}) copy-start(s32[5]{0:T(128)} %param.17) | copy-start | bytes 64
  6.5 31.1 %copy-start.4 = (bf16[4,5,576]{2,0,1:T(4,128)(2,1)S(1)}, bf16[4,5,576]{2,0,1:T(4,128)(2,1)}, u32[]{:S(2)}) copy-start(bf16[4,5,576]{2,0,1:T(4,128)(2,1)} %param.13) | copy-start | bytes 69124
  6.5 56.7 %all-gather.4.cloned.1.call-start = ((), (), s32[]{:S(2)}) async-start(), calls=%async_computation.3 | async-start | bytes 2162688 | tf_op jit(solution)/shard_map/all_gather | solution.py:73
  16.7 92.1 %all-gather.8.cloned.1.call-start = ((), (), s32[]{:S(2)}) async-start(), calls=%async_computation.5 | async-start | bytes 2162688 | tf_op jit(solution)/shard_map/all_gather | solution.py:74
  25.2 140.6 %all-gather.6.cloned.1.call-start = ((), (), s32[]{:S(2)}) async-start(), calls=%async_computation.4 | async-start | bytes 9732096 | tf_op jit(solution)/shard_map/all_gather | solution.py:87
  202.8 27.6 %copy-start.1 = (bf16[320,4096]{1,0:T(8,128)(2,1)S(1)}, bf16[320,4096]{1,0:T(8,128)(2,1)}, u32[]{:S(2)}) copy-start(bf16[320,4096]{1,0:T(8,128)(2,1)} %param.15) | copy-start | bytes 7864324
  231.2 9.7 %copy-start.2 = (s32[1024]{0:T(1024)}, s32[1024]{0:T(1024)S(1)}, u32[]{:S(2)}) copy-start(s32[1024]{0:T(1024)S(1)} %pad_clamp_fusion.3) | copy-start | bytes 12292 | tf_op jit(solution)/shard_map/while
  248.6 7.3 %copy-start = (bf16[64,64,512]{2,1,0:T(8,128)(2,1)S(1)}, bf16[64,64,512]{2,1,0:T(8,128)(2,1)}, u32[]{:S(2)}) copy-start(bf16[64,64,512]{2,1,0:T(8,128)(2,1)} %gather_fusion) | copy-start | bytes 12582916 | tf_op jit(solution)/shard_map/while
  258.0 9.7 %copy-start.2 = (s32[1024]{0:T(1024)}, s32[1024]{0:T(1024)S(1)}, u32[]{:S(2)}) copy-start(s32[1024]{0:T(1024)S(1)} %pad_clamp_fusion.3) | copy-start | bytes 12292 | tf_op jit(solution)/shard_map/while
  275.4 7.2 %copy-start = (bf16[64,64,512]{2,1,0:T(8,128)(2,1)S(1)}, bf16[64,64,512]{2,1,0:T(8,128)(2,1)}, u32[]{:S(2)}) copy-start(bf16[64,64,512]{2,1,0:T(8,128)(2,1)} %gather_fusion) | copy-start | bytes 12582916 | tf_op jit(solution)/shard_map/while
  284.8 9.7 %copy-start.2 = (s32[1024]{0:T(1024)}, s32[1024]{0:T(1024)S(1)}, u32[]{:S(2)}) copy-start(s32[1024]{0:T(1024)S(1)} %pad_clamp_fusion.3) | copy-start | bytes 12292 | tf_op jit(solution)/shard_map/while
  302.2 7.2 %copy-start = (bf16[64,64,512]{2,1,0:T(8,128)(2,1)S(1)}, bf16[64,64,512]{2,1,0:T(8,128)(2,1)}, u32[]{:S(2)}) copy-start(bf16[64,64,512]{2,1,0:T(8,128)(2,1)} %gather_fusion) | copy-start | bytes 12582916 | tf_op jit(solution)/shard_map/while
  311.6 9.7 %copy-start.2 = (s32[1024]{0:T(1024)}, s32[1024]{0:T(1024)S(1)}, u32[]{:S(2)}) copy-start(s32[1024]{0:T(1024)S(1)} %pad_clamp_fusion.3) | copy-start | bytes 12292 | tf_op jit(solution)/shard_map/while
  328.9 7.3 %copy-start = (bf16[64,64,512]{2,1,0:T(8,128)(2,1)S(1)}, bf16[64,64,512]{2,1,0:T(8,128)(2,1)}, u32[]{:S(2)}) copy-start(bf16[64,64,512]{2,1,0:T(8,128)(2,1)} %gather_fusion) | copy-start | bytes 12582916 | tf_op jit(solution)/shard_map/while
  338.4 9.7 %copy-start.2 = (s32[1024]{0:T(1024)}, s32[1024]{0:T(1024)S(1)}, u32[]{:S(2)}) copy-start(s32[1024]{0:T(1024)S(1)} %pad_clamp_fusion.3) | copy-start | bytes 12292 | tf_op jit(solution)/shard_map/while
  355.8 7.2 %copy-start = (bf16[64,64,512]{2,1,0:T(8,128)(2,1)S(1)}, bf16[64,64,512]{2,1,0:T(8,128)(2,1)}, u32[]{:S(2)}) copy-start(bf16[64,64,512]{2,1,0:T(8,128)(2,1)} %gather_fusion) | copy-start | bytes 12582916 | tf_op jit(solution)/shard_map/while
Sparse Core Ops, SparseCore 0:
  16.8 46.3 all-gather.3
  65.5 43.2 all-gather.7
  111.0 54.7 all-gather.5
where the time goes:
time: 376 us; the launch traced here: 374 us
  waiting for transfers between devices  120 us (32%)
  matrix products  107 us (28%)
  local copies, waits for them, and re-layouts  97.1 us (26%)
  blocking collectives  25.8 us (7%)
  between operations  13.3 us (4%)
  other arithmetic  10.8 us (3%)
    all_gather x1, waiting for transfers between devices, on_device(): shard_rows = lax.all_gather(part_query, 'rep', axis=0, tiled=True)  53.1 us
    gather x5, local copies, waits for them, and re-layouts, one_request(): latent = cache_latent[page_ids].reshape(slot_count, LAT)  48.7 us
    all_gather x1, waiting for transfers between devices, on_device(): lax.all_gather(part_value, 'rep', axis=0, tiled=True)  42.7 us
    dot_general x1, matrix products, on_device(): jnp.einsum('rn,nhl->rhl', ordered_wide, absorbed, precision=highest)  27.5 us
    all_gather x1, waiting for transfers between devices, on_device(): lax.all_gather(part_key, 'rep', axis=0, tiled=True)  23.8 us
    dot_general x5, matrix products, attend_request(): jnp.einsum('shl,tl->sht', query_lat, latent, preferred_element_type=jnp.f...  22.7 us
    dot_general x1, matrix products, on_device(): jnp.einsum('nhd,lhd->nhl', divided[:, :, :DN], key_heads, preferred_eleme...  20.6 us
    all_gather x1, local copies, waits for them, and re-layouts, on_device(): shard_rows = lax.all_gather(part_query, 'rep', axis=0, tiled=True)  12.7 us
  transfers between devices with their start and end apart: 3, of which 3 were waited for; matrix products, arithmetic and copies ran while one was open for 3% of the time, Pallas kernels for 0%

commit v1 on v0

v1 whole, which is shorter than its diff:
```python
import functools

import jax
import jax.numpy as jnp
import numpy as np
from jax import lax
from jax.experimental import pallas as pl
from jax.experimental.pallas import tpu as pltpu
from jax.sharding import PartitionSpec as P

LAT = 512
DN = 128
DR = 64
STEPS = 4
REQ = 5
POOL = 320
QR = 1536
HEADS = 16
GROUP = 16
REP = 32
XN = 4
TAIL = QR // 4
XW = QR + TAIL
MSG = 96
QW = 896
SCALE = float((DN + DR) ** -0.5 * np.log2(np.e))
NEG = -1e30
MESH = pl.DeviceIdType.MESH
F32 = jnp.float32
BF16 = jnp.bfloat16
NT = (((1,), (1,)), ((), ()))


def iota(shape, dim):
    return lax.broadcasted_iota(jnp.int32, shape, dim)


def kernel(
    x_ref, ne_ref, lat_hbm, rope_hbm, bt, ln, own, wq_hbm, wk_hbm, wv_hbm, freq_ref, out_ref,
    pool, zpool, rope, wx, kx, vx, wf, kf, msend, mrecv, vfull, xs, xsend, xrecv, xexp, wall,
    qsend, qrecv, wqt, s_a, s_b, m_sc, l_sc, acc, att, nef, cs, pick, outf, inv,
    sem_local, sem_own, a_send, a_recv, x_send, x_recv, xc_sem, m_send, m_recv,
    v_send, v_recv, vc_sem, q_send, q_recv,
):
    r = lax.axis_index("rep")
    hx = lax.axis_index("head")
    core = lax.rem(r, 2)
    chip = r // 2
    base = (r // GROUP) * GROUP
    mine = lax.rem(r, GROUP)
    cell = mine // 2
    other = r + 1 - 2 * core

    rope_copy = pltpu.make_async_copy(rope_hbm, rope, sem_local.at[0])
    rope_copy.start()
    pool_copy = pltpu.make_async_copy(lat_hbm, pool, sem_local.at[1])
    pool_copy.start()

    barrier = pltpu.get_barrier_semaphore()
    for k in range(1, XN):
        pl.semaphore_signal(barrier, inc=1, device_id={"head": lax.rem(hx + k, XN)}, device_id_type=MESH)

    def greet(k, _):
        pl.semaphore_signal(barrier, inc=1, device_id={"rep": lax.rem(r + k, REP)}, device_id_type=MESH)
        return 0

    lax.fori_loop(1, REP, greet, 0)

    for s in range(STEPS):
        row = x_ref[s].astype(F32)
        for i in range(4):
            xs[i * 4 + s : i * 4 + s + 1, :QR] = row[i : i + 1]
        for j in range(4):
            xs[4 * j + s : 4 * j + s + 1, QR:] = row[4:5, TAIL * j : TAIL * (j + 1)]
    xsend[...] = xs[...].astype(BF16)

    pl.semaphore_wait(barrier, XN - 1 + REP - 1)

    parts = ((wq_hbm, wx, 3072), (wk_hbm, kx, 2048), (wv_hbm, vx, 2048))

    def a_copy(n, k):
        src, dst, width = parts[n]
        to = lax.rem(hx + k, XN)
        return pltpu.make_async_remote_copy(
            src_ref=src.at[:, pl.ds(pl.multiple_of(to * width, 128), width)],
            dst_ref=dst.at[hx],
            send_sem=a_send.at[n, k],
            recv_sem=a_recv.at[n, hx],
            device_id={"head": to},
            device_id_type=MESH,
        )

    def a_wait(n, k):
        src, dst, width = parts[n]
        frm = lax.rem(hx + k, XN)
        pltpu.make_async_remote_copy(
            src_ref=dst.at[frm], dst_ref=dst.at[frm], send_sem=a_send.at[n, k], recv_sem=a_recv.at[n, frm],
            device_id={"head": frm}, device_id_type=MESH,
        ).wait_recv()

    def own_copy(n):
        src, dst, width = parts[n]
        return pltpu.make_async_copy(
            src.at[:, pl.ds(pl.multiple_of(hx * width, 128), width)], dst.at[hx], sem_own.at[n]
        )

    for n in range(3):
        for k in (2, 1, 3):
            a_copy(n, k).start()
        own_copy(n).start()

    def x_copy(k):
        to = lax.rem(cell + k, 8)
        return pltpu.make_async_remote_copy(
            src_ref=xsend, dst_ref=xrecv.at[cell, core], send_sem=x_send.at[k], recv_sem=x_recv.at[cell],
            device_id={"rep": base + 2 * to + core}, device_id_type=MESH,
        )

    def x_start(k, _):
        x_copy(k).start()
        return 0

    lax.fori_loop(1, 8, x_start, 0)
    xrecv[cell, core] = xsend[...]

    def invert(j, _):
        at = jnp.int32(0)
        for n in range(REP):
            at = jnp.where(own[n] == j, jnp.int32(n), at)
        inv[j] = at
        return 0

    lax.fori_loop(0, REP, invert, 0)

    lane8 = iota((8, 128), 1)
    sub8 = iota((8, 128), 0)
    sign = jnp.where(lax.rem(lane8, DR) < DR // 2, -1.0, 1.0).astype(F32)
    for i in range(REQ):
        angle = (ln[i] + lax.rem(sub8, STEPS)).astype(F32) * freq_ref[...]
        cs[i, 0] = jnp.cos(angle)
        cs[i, 1] = jnp.sin(angle) * sign
    nef[...] = jnp.zeros_like(nef)
    for u in range(STEPS):
        row = ne_ref[u].astype(F32)
        for i in range(REQ):
            nef[i, u : u + 1, : LAT + DR] = row[i : i + 1]
    for i in range(REQ):
        v = nef[i, :, LAT:]
        v = v + pltpu.roll(v, DR, 1)
        v = v * cs[i, 0] + pltpu.roll(v, DR // 2, 1) * cs[i, 1]
        nef[i, :, LAT:] = jnp.where(lane8 < DR, v, 0.0)

    def clear(n, _):
        wqt[n // 9, pl.ds(pl.multiple_of(lax.rem(n, 9) * 256, 256), 256), :] = jnp.zeros((256, 256), BF16)
        return 0

    lax.fori_loop(0, REQ * 9, clear, 0)
    prow = iota((1024, 512), 0)
    pcol = iota((1024, 512), 1)
    pick[...] = jnp.where(
        (pcol // 16 == lax.rem(prow, 64) // 2) & (lax.rem(pcol, 16) == prow // 64), 1.0, 0.0
    ).astype(BF16)

    rope_copy.wait()

    def rope_step(n, _):
        a, b = n // 4, lax.rem(n, 4)
        top = pl.multiple_of(a * 32, 32)
        cat = jnp.concatenate(
            [
                jnp.concatenate(
                    [rope[pl.ds(top, 16), 128 * j : 128 * j + 128], rope[pl.ds(top + 16, 16), 128 * j : 128 * j + 128]],
                    axis=1,
                )
                for j in range(32)
            ],
            axis=0,
        )
        got = jnp.dot(pick[pl.ds(pl.multiple_of(b * 256, 256), 256), :], cat, preferred_element_type=F32)
        keep = (iota((256, 128), 1) < DR) == (lax.rem(iota((256, 128), 0), 2) == 0)
        for g in range(2):
            v = got[:, 128 * g : 128 * g + 128]
            v = jnp.where(keep, v, pltpu.roll(v, DR, 1)).astype(BF16)
            zpool[pl.ds(a * 32 + g * 16 + b * 4, 4)] = v.reshape(4, 64, 128)
        return 0

    lax.fori_loop(0, 40, rope_step, 0)

    for n in range(2):
        own_copy(n).wait()
        for k in range(1, XN):
            a_wait(n, k)
    for k in range(XN):
        wf[12 * k : 12 * k + 12, :] = wx[k].astype(F32)
        kf[4 * k : 4 * k + 4, :] = kx[k].astype(F32)
    low48 = iota((48, 128), 1) < DR
    low24 = iota((24, 128), 1) < DR
    for p in range(HEADS // 2):
        first = wf[:, 384 * p : 384 * p + 128]
        mid = wf[:, 384 * p + 128 : 384 * p + 256]
        last = wf[:, 384 * p + 256 : 384 * p + 384]
        mid_r = pltpu.roll(mid, DR, 1)
        last_r = pltpu.roll(last, DR, 1)
        msend[2 * p, 0:48] = first.astype(BF16)
        msend[2 * p + 1, 0:48] = jnp.where(low48, mid_r, last_r).astype(BF16)
        pad = jnp.zeros((8, 128), F32)
        even = jnp.concatenate([jnp.where(low24, mid[:24], mid_r[24:]), pad], axis=0)
        odd = jnp.concatenate([jnp.where(low24, last_r[:24], last[24:]), pad], axis=0)
        msend[2 * p, 64:96] = even.astype(BF16)
        msend[2 * p + 1, 64:96] = odd.astype(BF16)
        for g in range(2):
            h = 2 * p + g
            msend[h, 48:64] = kf[:, 128 * h : 128 * h + 128].astype(BF16)

    def m_copy(k):
        to = lax.rem(r + k, REP)
        return pltpu.make_async_remote_copy(
            src_ref=msend.at[lax.rem(to, GROUP)], dst_ref=mrecv.at[r], send_sem=m_send.at[k], recv_sem=m_recv.at[r],
            device_id={"rep": to}, device_id_type=MESH,
        )

    def m_start(k, _):
        m_copy(k).start()
        return 0

    lax.fori_loop(1, REP, m_start, 0)
    mrecv[r] = msend[mine]

    def x_wait(k, _):
        frm = lax.rem(cell + k, 8)
        pltpu.make_async_remote_copy(
            src_ref=xsend, dst_ref=xrecv.at[frm, core], send_sem=x_send.at[k], recv_sem=x_recv.at[frm],
            device_id={"rep": base + 2 * frm + core}, device_id_type=MESH,
        ).wait_recv()
        return 0

    lax.fori_loop(1, 8, x_wait, 0)
    xc = pltpu.make_async_remote_copy(
        src_ref=xrecv.at[:, core], dst_ref=xrecv.at[:, core], send_sem=xc_sem.at[0], recv_sem=xc_sem.at[1],
        device_id={"rep": other}, device_id_type=MESH,
    )
    xc.start()

    own_copy(2).wait()
    for k in range(1, XN):
        a_wait(2, k)
    for k in range(XN):
        kf[4 * k : 4 * k + 4, :] = vx[k].astype(F32)
    vfull[chip, core] = kf[...].astype(BF16)

    def v_copy(k):
        to = lax.rem(chip + k, 16)
        return pltpu.make_async_remote_copy(
            src_ref=vfull.at[chip, core], dst_ref=vfull.at[chip, core], send_sem=v_send.at[k], recv_sem=v_recv.at[chip],
            device_id={"rep": 2 * to + core}, device_id_type=MESH,
        )

    pltpu.make_async_remote_copy(
        src_ref=xrecv.at[:, 1 - core], dst_ref=xrecv.at[:, 1 - core], send_sem=xc_sem.at[0], recv_sem=xc_sem.at[1],
        device_id={"rep": other}, device_id_type=MESH,
    ).wait_recv()

    def spread(n, _):
        got = xrecv[n // 2, lax.rem(n, 2)]
        xexp[n, 0:16, :] = got[:, :QR]
        for j in range(4):
            mask = jnp.where(iota((16, TAIL), 0) // 4 == j, 1.0, 0.0).astype(BF16)
            xexp[n, 16:32, TAIL * j : TAIL * (j + 1)] = got[:, QR:] * mask
        return 0

    lax.fori_loop(0, GROUP, spread, 0)

    def m_wait(k, _):
        frm = lax.rem(r + k, REP)
        pltpu.make_async_remote_copy(
            src_ref=mrecv.at[frm], dst_ref=mrecv.at[frm], send_sem=m_send.at[k], recv_sem=m_recv.at[frm],
            device_id={"rep": frm}, device_id_type=MESH,
        ).wait_recv()
        return 0

    lax.fori_loop(1, REP, m_wait, 0)

    def place(j, _):
        block = mrecv[inv[j]]
        rows = pl.ds(pl.multiple_of(j * 48, 16), 48)
        wall[rows, 0:128] = block[0:48]
        t = block[64:96].astype(F32)[:24]
        t_r = pltpu.roll(t, DR, 1)
        low = iota((24, 128), 1) < DR
        both = jnp.concatenate([jnp.where(low, t, t_r), jnp.where(low, t_r, t)], axis=0)
        wall[rows, 128:256] = both.astype(BF16)
        return 0

    lax.fori_loop(0, REP, place, 0)

    raw = jnp.dot(xexp[...].reshape(GROUP * 32, QR), wall[...], preferred_element_type=F32).reshape(GROUP, 32, 256)
    tail = raw[:, 16:24] + raw[:, 24:32]
    tail = tail + jnp.concatenate([tail[:, 4:8], tail[:, 0:4]], axis=1)
    main = raw[:, 0:16].reshape(GROUP * 16, 256)
    tail = tail.reshape(GROUP * 8, 256)
    both = jnp.concatenate([main, tail], axis=0)
    nope = both[:, :128]
    hi = nope.astype(BF16)
    lo = (nope - hi.astype(F32)).astype(BF16)
    key = mrecv[:, 48:64, :].reshape(LAT, 128)
    lat = lax.dot_general(
        jnp.concatenate([hi, lo], axis=1), jnp.concatenate([key, key], axis=1), NT, preferred_element_type=F32
    )
    rot = both[:, 128:]
    rot_hi = rot.astype(BF16).astype(F32)
    rot = jnp.where(iota(rot.shape, 1) < DR, rot_hi, rot - rot_hi)
    nmain = GROUP * 16
    qsend[:, :, 0:512] = lat[:nmain].astype(BF16).reshape(GROUP, 16, 512)
    qsend[:, :, 512:640] = rot[:nmain].astype(BF16).reshape(GROUP, 16, 128)
    ltail = lat[nmain:].reshape(GROUP, 8, 512)
    upper = iota((GROUP, 8, 128), 1) < 4
    pair = [
        jnp.where(upper, ltail[:, :, 256 * n : 256 * n + 128], ltail[:, :, 256 * n + 128 : 256 * n + 256])
        for n in range(2)
    ]
    qsend[:, :, 640:768] = jnp.concatenate(pair, axis=1).astype(BF16)
    rtail = rot[nmain:].reshape(GROUP, 8, 128)
    qsend[:, :, 768:896] = jnp.concatenate([rtail, rtail], axis=1).astype(BF16)

    def q_copy(k):
        to = lax.rem(mine + k, GROUP)
        return pltpu.make_async_remote_copy(
            src_ref=qsend.at[to], dst_ref=qrecv.at[mine], send_sem=q_send.at[k], recv_sem=q_recv.at[mine],
            device_id={"rep": base + to}, device_id_type=MESH,
        )

    def q_start(k, _):
        q_copy(k).start()
        return 0

    lax.fori_loop(1, GROUP, q_start, 0)
    qrecv[mine] = qsend[mine]

    def v_start(k, _):
        v_copy(k).start()
        return 0

    lax.fori_loop(1, 16, v_start, 0)

    perm_row = iota((256, 256), 0)
    want = lax.rem(perm_row // 4, 16) * 16 + (perm_row // 64) * 4 + lax.rem(perm_row, 4)
    perm = jnp.where(iota((256, 256), 1) == want, 1.0, 0.0).astype(BF16)

    def q_wait(k, _):
        frm = lax.rem(mine + k, GROUP)
        pltpu.make_async_remote_copy(
            src_ref=qsend.at[frm], dst_ref=qrecv.at[frm], send_sem=q_send.at[k], recv_sem=q_recv.at[frm],
            device_id={"rep": base + frm}, device_id_type=MESH,
        ).wait_recv()
        return 0

    lax.fori_loop(1, GROUP, q_wait, 0)

    low_q = iota((LAT, 128), 1) < DR
    low_r = iota((DR, 128), 1) < DR
    got = jnp.dot(perm, qrecv[...].reshape(GROUP * 16, QW), preferred_element_type=F32)
    for i in range(REQ):
        if i < 4:
            lat_i = got[64 * i : 64 * i + 64, :512]
            rp = got[64 * i : 64 * i + 64, 512:640]
        else:
            lat_i = jnp.concatenate([got[64 * j : 64 * j + 64, 640:768] for j in range(4)], axis=1)
            rp = got[0:64, 768:896]
        rr = rp + pltpu.roll(rp, DR, 1)
        cos = jnp.concatenate([cs[i, 0]] * 8, axis=0)
        sin = jnp.concatenate([cs[i, 1]] * 8, axis=0)
        rr = rr * cos + pltpu.roll(rr, DR // 2, 1) * sin
        lat_t = jnp.transpose(jnp.concatenate([lat_i, lat_i], axis=0))
        rr_t = jnp.transpose(jnp.concatenate([rr, rr], axis=0))[:DR]
        left = jnp.where(low_q, lat_t, 0.0).astype(BF16)
        right = jnp.where(low_q, 0.0, lat_t).astype(BF16)
        rleft = jnp.where(low_r, rr_t, 0.0).astype(BF16)
        rright = jnp.where(low_r, 0.0, rr_t).astype(BF16)
        wqt[i, 0:512, 0:128] = left
        wqt[i, 512:1024, 0:128] = right
        wqt[i, 1024:1536, 128:256] = left
        wqt[i, 1536:2048, 128:256] = right
        wqt[i, 2048:2112, 0:128] = rleft
        wqt[i, 2112:2176, 0:128] = rright
        wqt[i, 2176:2240, 128:256] = rleft
        wqt[i, 2240:2304, 128:256] = rright

    pool_copy.wait()

    def page(i, c, k, g):
        return bt[i, c * 16 + k * 4 + g]

    def keys(i, c, k):
        return jnp.concatenate([pool[page(i, c, k, g)] for g in range(4)], axis=0)

    def scores(i, buf, slot):
        def chunk(c):
            s = jnp.dot(keys(i, c, 0), wqt[i, 0:512], preferred_element_type=F32)
            for k in range(1, 4):
                s = s + jnp.dot(keys(i, c, k), wqt[i, 512 * k : 512 * k + 512], preferred_element_type=F32)
            low = iota((64, 128), 1) < DR
            rows = []
            for g in range(4):
                rows.append(
                    jnp.concatenate(
                        [
                            jnp.where(low, zpool[page(i, c, 2 * e, g)], zpool[page(i, c, 2 * e + 1, g)])
                            for e in range(2)
                        ],
                        axis=1,
                    )
                )
            s = s + jnp.dot(jnp.concatenate(rows, axis=0), wqt[i, 2048:2304], preferred_element_type=F32)
            token = iota((256, 256), 0) + (iota((256, 256), 1) // 64) * 256
            s = jnp.where(token < ln[i] - c * 1024, s, NEG)
            buf[pl.ds(pl.multiple_of(c * 256, 256), 256), :] = s
            m_sc[slot] = jnp.maximum(m_sc[slot], jnp.max(s.reshape(32, 8, 256), axis=0))

        return chunk

    def fresh(i, buf, slot):
        new = jnp.concatenate([nef[i], jnp.zeros((8, 640), F32)], axis=0).astype(BF16)
        s = jnp.dot(new[:, :LAT], wqt[i, 0:512], preferred_element_type=F32)
        s = s + jnp.dot(new[:, LAT:], wqt[i, 2048:2176], preferred_element_type=F32)
        u = iota((16, 256), 0)
        lane = iota((16, 256), 1)
        s = jnp.where((lane < 64) & (u <= lax.rem(lane, STEPS)), s, NEG)
        buf[1024:1040, :] = s
        m_sc[slot] = jnp.maximum(s[0:8], s[8:16])

    def top(slot):
        m = jnp.max(m_sc[slot], axis=0, keepdims=True)
        m = jnp.broadcast_to(m, (8, 256))
        m = jnp.maximum(m, pltpu.roll(m, 128, 1))
        m = jnp.maximum(m, pltpu.roll(m, 64, 1))
        return m

    def weigh(i, buf, slot):
        def chunk(c):
            s = buf[pl.ds(pl.multiple_of(c * 256, 256), 256), :]
            p = jnp.exp2((s - m_sc[slot][0:1]) * SCALE)
            l_sc[...] = l_sc[...] + jnp.sum(p.reshape(32, 8, 256), axis=0)
            pt = jnp.transpose(p).astype(BF16)
            t = acc[...]
            for k in range(4):
                t = t + jnp.dot(pt[64 * k : 64 * k + 64], keys(i, c, k), preferred_element_type=F32)
            acc[...] = t

        return chunk

    def weigh_fresh(i, buf, slot):
        s = buf[1024:1040, :]
        p = jnp.exp2((s - m_sc[slot][0:1]) * SCALE)
        l_sc[...] = p[0:8] + p[8:16]
        pt = jnp.transpose(jnp.concatenate([p[:, 0:128], jnp.zeros((112, 128), F32)], axis=0)).astype(BF16)
        new = jnp.concatenate([nef[i, :, :LAT], jnp.zeros((120, LAT), F32)], axis=0).astype(BF16)
        acc[...] = jnp.dot(pt[:64], new, preferred_element_type=F32)

    def finish(i):
        total = jnp.sum(l_sc[...], axis=0, keepdims=True)
        total = jnp.broadcast_to(total, (8, 256))
        total = total + pltpu.roll(total, 128, 1)
        total = total + pltpu.roll(total, 64, 1)
        col = jnp.transpose(jnp.broadcast_to(1.0 / total[0:1, :128], (128, 128)))[:64, 0:1]
        att[i] = acc[...] * col

    def forward():
        def v_wait(k, _):
            frm = lax.rem(chip + k, 16)
            pltpu.make_async_remote_copy(
                src_ref=vfull.at[frm, core], dst_ref=vfull.at[frm, core], send_sem=v_send.at[k],
                recv_sem=v_recv.at[frm], device_id={"rep": 2 * frm + core}, device_id_type=MESH,
            ).wait_recv()
            return 0

        lax.fori_loop(1, 16, v_wait, 0)
        pltpu.make_async_remote_copy(
            src_ref=vfull.at[:, core], dst_ref=vfull.at[:, core], send_sem=vc_sem.at[0], recv_sem=vc_sem.at[1],
            device_id={"rep": other}, device_id_type=MESH,
        ).start()

    bufs = (s_a, s_b)
    for i in range(REQ + 1):
        if i < REQ:
            fresh(i, bufs[i % 2], i % 2)
        if i > 0:
            m_sc[(i - 1) % 2] = top((i - 1) % 2)
            weigh_fresh(i - 1, bufs[(i - 1) % 2], (i - 1) % 2)

        def step(c, _, i=i):
            if i < REQ:
                scores(i, bufs[i % 2], i % 2)(c)
            if i > 0:
                weigh(i - 1, bufs[(i - 1) % 2], (i - 1) % 2)(c)
            return 0

        lax.fori_loop(0, 4, step, 0)
        if i > 0:
            finish(i - 1)
        if i == 3:
            forward()

    pltpu.make_async_remote_copy(
        src_ref=vfull.at[:, 1 - core], dst_ref=vfull.at[:, 1 - core], send_sem=vc_sem.at[0], recv_sem=vc_sem.at[1],
        device_id={"rep": other}, device_id_type=MESH,
    ).wait_recv()
    for p in range(HEADS // 2):
        rows = att[:, 8 * p : 8 * p + 8, :].reshape(REQ * 8, LAT).astype(BF16)
        v = vfull[:, :, :, 256 * p : 256 * p + 256].reshape(LAT, 256)
        o = jnp.dot(rows, v, preferred_element_type=F32).reshape(REQ, 8, 256)
        for i in range(REQ):
            for s in range(STEPS):
                outf[s, i : i + 1, 256 * p : 256 * p + 128] = o[i, s : s + 1, 0:128]
                outf[s, i : i + 1, 256 * p + 128 : 256 * p + 256] = o[i, 4 + s : 5 + s, 128:256]
    for s in range(STEPS):
        out_ref[s] = outf[s, 0:REQ].astype(BF16)

    for n in range(3):
        for k in range(1, XN):
            a_copy(n, k).wait_send()

    def drain(k, _):
        x_copy(k).wait_send()
        return 0

    lax.fori_loop(1, 8, drain, 0)
    xc.wait_send()

    def drain_m(k, _):
        m_copy(k).wait_send()
        return 0

    lax.fori_loop(1, REP, drain_m, 0)

    def drain_qv(k, _):
        q_copy(k).wait_send()
        v_copy(k).wait_send()
        return 0

    lax.fori_loop(1, 16, drain_qv, 0)
    pltpu.make_async_remote_copy(
        src_ref=vfull.at[:, core], dst_ref=vfull.at[:, core], send_sem=vc_sem.at[0], recv_sem=vc_sem.at[1],
        device_id={"rep": other}, device_id_type=MESH,
    ).wait_send()


def on_device(query_latent, new_entry, cache_latent, cache_rope, block_table, context_len, owner_rows, query_up, key_up, value_up):
    half = DR // 2
    freq = np.float32(10000.0) ** (-np.arange(half, dtype=np.float32) / np.float32(half))
    freq = jnp.asarray(np.tile(freq, 4).reshape(1, 128).astype(np.float32))
    vmem = pl.BlockSpec(memory_space=pltpu.VMEM)
    smem = pl.BlockSpec(memory_space=pltpu.SMEM)
    hbm = pl.BlockSpec(memory_space=pl.ANY)
    dma = pltpu.SemaphoreType.DMA
    return pl.pallas_call(
        kernel,
        out_shape=jax.ShapeDtypeStruct((STEPS, REQ, HEADS * DN), BF16),
        in_specs=[vmem, vmem, hbm, hbm, smem, smem, smem, hbm, hbm, hbm, vmem],
        out_specs=vmem,
        scratch_shapes=[
            pltpu.VMEM((POOL, 64, LAT), BF16),
            pltpu.VMEM((POOL, 64, 128), BF16),
            pltpu.VMEM((POOL, 4096), BF16),
            pltpu.VMEM((XN, 12, 3072), BF16),
            pltpu.VMEM((XN, 4, 2048), BF16),
            pltpu.VMEM((XN, 4, 2048), BF16),
            pltpu.VMEM((48, 3072), F32),
            pltpu.VMEM((16, 2048), F32),
            pltpu.VMEM((HEADS, MSG, 128), BF16),
            pltpu.VMEM((REP, MSG, 128), BF16),
            pltpu.VMEM((16, 2, 16, 2048), BF16),
            pltpu.VMEM((16, XW), F32),
            pltpu.VMEM((16, XW), BF16),
            pltpu.VMEM((8, 2, 16, XW), BF16),
            pltpu.VMEM((GROUP, 32, QR), BF16),
            pltpu.VMEM((QR, 256), BF16),
            pltpu.VMEM((GROUP, 16, QW), BF16),
            pltpu.VMEM((GROUP, 16, QW), BF16),
            pltpu.VMEM((REQ, 2304, 256), BF16),
            pltpu.VMEM((1040, 256), F32),
            pltpu.VMEM((1040, 256), F32),
            pltpu.VMEM((2, 8, 256), F32),
            pltpu.VMEM((8, 256), F32),
            pltpu.VMEM((64, LAT), F32),
            pltpu.VMEM((REQ, 64, LAT), F32),
            pltpu.VMEM((REQ, 8, 640), F32),
            pltpu.VMEM((REQ, 2, 8, 128), F32),
            pltpu.VMEM((1024, 512), BF16),
            pltpu.VMEM((STEPS, 8, HEADS * DN), F32),
            pltpu.SMEM((REP,), jnp.int32),
            dma((2,)), dma((3,)), dma((3, XN)), dma((3, XN)),
            dma((8,)), dma((8,)), dma((2,)), dma((REP,)), dma((REP,)),
            dma((16,)), dma((16,)), dma((2,)), dma((GROUP,)), dma((GROUP,)),
        ],
        compiler_params=pltpu.CompilerParams(
            collective_id=0, has_side_effects=True, vmem_limit_bytes=60 * 2**20
        ),
        name="latent_attention",
    )(query_latent, new_entry, cache_latent, cache_rope, block_table, context_len, owner_rows, query_up, key_up, value_up, freq)


def solution(mesh):
    return jax.shard_map(
        on_device,
        mesh=mesh,
        in_specs=(
            P(None, "rep", None),
            P(None, "rep", None),
            P("rep", None, None),
            P("rep", None),
            P("rep", None),
            P("rep"),
            P(),
            P(("rep", "head"), None),
            P(("rep", "head"), None),
            P(("rep", "head"), None),
        ),
        out_specs=P(None, "rep", "head"),
        check_vma=False,
    )
```

time: 376 us -> 72.5 us (0.19)
  waiting for transfers between devices: 120 us -> 0 us
  matrix products: 107 us -> 0 us
  local copies, waits for them, and re-layouts: 97.1 us -> 4.46 us
  Pallas kernels: 0 us -> 67.8 us
  blocking collectives: 25.8 us -> 0 us
  between operations: 13.3 us -> 0.01 us
  other arithmetic: 10.8 us -> 0 us
    all_gather x3 -> x0, waiting for transfers between devices: 120 us -> none  [the longest x1 53.1 us: on_device(): shard_rows = lax.all_gather(part_query, 'rep', axis=0, tiled=True)]
    dot_general x34 -> x0, matrix products: 107 us -> none  [the longest x1 27.5 us: on_device(): jnp.einsum('rn,nhl->rhl', ordered_wide, absorbed, precision=highest)]
    pallas_call x0 -> x1, Pallas kernels: none -> 67.8 us  [on_device(): pl.pallas_call(kernel, out_shape=jax.ShapeDtypeStruct((STEPS, REQ, HEADS...]
    gather x15 -> x0, local copies, waits for them, and re-layouts: 54.9 us -> none  [the longest x5 48.7 us: one_request(): latent = cache_latent[page_ids].reshape(slot_count, LAT)]
    all_to_all x3 -> x0, blocking collectives: 25.8 us -> none  [the longest x1 9.46 us: on_device(): lax.all_to_all(key_up, 'head', split_axis=1, concat_axis=0, tiled=True)]
    all_gather x3 -> x0, local copies, waits for them, and re-layouts: 19.5 us -> none  [the longest x1 12.7 us: on_device(): shard_rows = lax.all_gather(part_query, 'rep', axis=0, tiled=True)]
    reshape x7 -> x0, local copies, waits for them, and re-layouts: 10.8 us -> none  [the longest x5 10.5 us: one_request(): rotary = cache_rope[page_ids].reshape(slot_count, DR)]
    dynamic_slice x5 -> x0, local copies, waits for them, and re-layouts: 6.93 us -> none  [on_device(): lax.map(one_request, (block_table, context_len, jnp.swapaxes(query_lat, 0...]
  transfers between devices with their start and end apart: 3 -> 0, of which waited for: 3 -> 0; matrix products, arithmetic and copies ran while one was open for 3% -> 0% of each run, Pallas kernels for 0% -> 0%
where the time goes in v1:
time: 72.5 us; the launch traced here: 72.3 us
  Pallas kernels  67.8 us (94%)
  local copies, waits for them, and re-layouts  4.46 us (6%)
    pallas_call x1, Pallas kernels, on_device(): pl.pallas_call(kernel, out_shape=jax.ShapeDtypeStruct((STEPS, REQ, HEADS...  67.8 us
    unnamed x2, local copies, waits for them, and re-layouts  2.84 us
    pallas_call x1, local copies, waits for them, and re-layouts, on_device(): pl.pallas_call(kernel, out_shape=jax.ShapeDtypeStruct((STEPS, REQ, HEADS...  1.61 us

profile of v1, /device:TPU:1, one launch (start us, length us, event | category | flops | bytes accessed | tf_op | source)
XLA Modules:
  0.0 72.3 jit_solution(13184800504421901579)
XLA Ops:
  0.0 1.4 %copy.13.ne_ref = bf16[4,5,576]{2,1,0:T(8,128)(2,1)} copy(bf16[4,5,576]{2,0,1:T(4,128)(2,1)} %param.12) | data formatting | bytes 46080 | tf_op args[1]
  1.4 1.5 %copy.12.x_ref = bf16[4,5,1536]{2,1,0:T(8,128)(2,1)} copy(bf16[4,5,1536]{2,0,1:T(4,128)(2,1)} %param.11) | data formatting | bytes 122880 | tf_op args[0]
  2.8 67.8 %latent_attention.1 = bf16[4,5,2048]{2,1,0:T(8,128)(2,1)} custom-call(bf16[4,5,1536]{2,1,0:T(8,128)(2,1)} %copy.12.x_ref, bf16[4,5,576]{2,1,0:T(8,128)(2,1)} %copy.13.ne_ref, bf16[320,64,512]{2,1,0:T(8,128)(2,1)} %lat_hbm.1, bf16[320,4096]{1,0:T(8,128)(2,1)} %rope_hbm.1, s32[5,64]{1,0:T(8,128)} %bt.1, s32[5]{0:T(128)} %ln.1, s32[32]{0:T(128)} %own.1, ...), custom_call_target="tpu_custom_call" | custom-call | tf_op jit(solution)/shard_map/latent_attention/pallas_call | solution.py:555
  70.7 1.6 %copy.14 = bf16[4,5,2048]{2,0,1:T(4,128)(2,1)} copy(bf16[4,5,2048]{2,1,0:T(8,128)(2,1)} %latent_attention.1) | data formatting | bytes 163840 | tf_op jit(solution)/shard_map/latent_attention/pallas_call | solution.py:555

commit v2 on v1

--- a/solution.py
+++ b/solution.py
@@ -25,6 +25,7 @@
 QW = 896
 SCALE = float((DN + DR) ** -0.5 * np.log2(np.e))
 NEG = -1e30
+UNROLL = 2
 MESH = pl.DeviceIdType.MESH
 F32 = jnp.float32
 BF16 = jnp.bfloat16
@@ -38,14 +39,15 @@
 def kernel(
     x_ref, ne_ref, lat_hbm, rope_hbm, bt, ln, own, wq_hbm, wk_hbm, wv_hbm, freq_ref, out_ref,
     pool, zpool, rope, wx, kx, vx, wf, kf, msend, mrecv, vfull, xs, xsend, xrecv, xexp, wall,
-    qsend, qrecv, wqt, s_a, s_b, m_sc, l_sc, acc, att, nef, cs, pick, outf, inv,
+    qsend, qrecv, wqt, s_a, s_b, m_sc, l_sc, acc, att, nef, cs, pick, inv,
     sem_local, sem_own, a_send, a_recv, x_send, x_recv, xc_sem, m_send, m_recv,
     v_send, v_recv, vc_sem, q_send, q_recv,
 ):
     r = lax.axis_index("rep")
     hx = lax.axis_index("head")
     core = lax.rem(r, 2)
-    chip = r // 2
+    zc = r // 8
+    yc = lax.rem(r // 2, 4)
     base = (r // GROUP) * GROUP
     mine = lax.rem(r, GROUP)
     cell = mine // 2
@@ -66,12 +68,11 @@
 
     lax.fori_loop(1, REP, greet, 0)
 
-    for s in range(STEPS):
-        row = x_ref[s].astype(F32)
-        for i in range(4):
-            xs[i * 4 + s : i * 4 + s + 1, :QR] = row[i : i + 1]
-        for j in range(4):
-            xs[4 * j + s : 4 * j + s + 1, QR:] = row[4:5, TAIL * j : TAIL * (j + 1)]
+    for i in range(4):
+        xs[4 * i : 4 * i + 4, :QR] = x_ref[i].astype(F32)
+    row = x_ref[4].astype(F32)
+    for j in range(4):
+        xs[4 * j : 4 * j + 4, QR:] = row[:, TAIL * j : TAIL * (j + 1)]
     xsend[...] = xs[...].astype(BF16)
 
     pl.semaphore_wait(barrier, XN - 1 + REP - 1)
@@ -140,11 +141,8 @@
         cs[i, 0] = jnp.cos(angle)
         cs[i, 1] = jnp.sin(angle) * sign
     nef[...] = jnp.zeros_like(nef)
-    for u in range(STEPS):
-        row = ne_ref[u].astype(F32)
-        for i in range(REQ):
-            nef[i, u : u + 1, : LAT + DR] = row[i : i + 1]
     for i in range(REQ):
+        nef[i, 0:STEPS, : LAT + DR] = ne_ref[i].astype(F32)
         v = nef[i, :, LAT:]
         v = v + pltpu.roll(v, DR, 1)
         v = v * cs[i, 0] + pltpu.roll(v, DR // 2, 1) * cs[i, 1]
@@ -161,10 +159,127 @@
         (pcol // 16 == lax.rem(prow, 64) // 2) & (lax.rem(pcol, 16) == prow // 64), 1.0, 0.0
     ).astype(BF16)
 
+    for n in range(2):
+        own_copy(n).wait()
+        for k in range(1, XN):
+            a_wait(n, k)
+    for k in range(XN):
+        wf[12 * k : 12 * k + 12, :] = wx[k].astype(F32)
+        kf[4 * k : 4 * k + 4, :] = kx[k].astype(F32)
+    low48 = iota((48, 128), 1) < DR
+    low24 = iota((24, 128), 1) < DR
+
+    def m_copy(h, half):
+        to = half * GROUP + h
+        return to, pltpu.make_async_remote_copy(
+            src_ref=msend.at[h], dst_ref=mrecv.at[r], send_sem=m_send.at[to], recv_sem=m_recv.at[r],
+            device_id={"rep": to}, device_id_type=MESH,
+        )
+
+    def make(k, _):
+        p = lax.rem(cell + k, HEADS // 2)
+        col = pl.multiple_of(p * 384, 128)
+        first = wf[:, pl.ds(col, 128)]
+        mid = wf[:, pl.ds(pl.multiple_of(col + 128, 128), 128)]
+        last = wf[:, pl.ds(pl.multiple_of(col + 256, 128), 128)]
+        mid_r = pltpu.roll(mid, DR, 1)
+        last_r = pltpu.roll(last, DR, 1)
+        pad = jnp.zeros((8, 128), F32)
+        even = jnp.concatenate([jnp.where(low24, mid[:24], mid_r[24:]), pad], axis=0)
+        odd = jnp.concatenate([jnp.where(low24, last_r[:24], last[24:]), pad], axis=0)
+        msend[2 * p, 0:48] = first.astype(BF16)
+        msend[2 * p, 48:64] = kf[:, pl.ds(pl.multiple_of(p * 256, 128), 128)].astype(BF16)
+        msend[2 * p, 64:96] = even.astype(BF16)
+        msend[2 * p + 1, 0:48] = jnp.where(low48, mid_r, last_r).astype(BF16)
+        msend[2 * p + 1, 48:64] = kf[:, pl.ds(pl.multiple_of(p * 256 + 128, 128), 128)].astype(BF16)
+        msend[2 * p + 1, 64:96] = odd.astype(BF16)
+        for g in range(2):
+            for half in range(2):
+                to, copy = m_copy(2 * p + g, half)
+
+                @pl.when(to != r)
+                def _(copy=copy):
+                    copy.start()
+
+        return 0
+
+    lax.fori_loop(0, HEADS // 2, make, 0)
+    mrecv[r] = msend[mine]
+
+    def x_wait(k, _):
+        frm = lax.rem(cell + k, 8)
+        pltpu.make_async_remote_copy(
+            src_ref=xsend, dst_ref=xrecv.at[frm, core], send_sem=x_send.at[k], recv_sem=x_recv.at[frm],
+            device_id={"rep": base + 2 * frm + core}, device_id_type=MESH,
+        ).wait_recv()
+        return 0
+
+    lax.fori_loop(1, 8, x_wait, 0)
+    xc = pltpu.make_async_remote_copy(
+        src_ref=xrecv.at[:, core], dst_ref=xrecv.at[:, core], send_sem=xc_sem.at[0], recv_sem=xc_sem.at[1],
+        device_id={"rep": other}, device_id_type=MESH,
+    )
+    xc.start()
+
+    own_copy(2).wait()
+    for k in range(1, XN):
+        a_wait(2, k)
+    for k in range(XN):
+        kf[4 * k : 4 * k + 4, :] = vx[k].astype(F32)
+    vfull[zc, yc, core] = kf[...].astype(BF16)
+
+    def v_peer(axis, k):
+        if axis == 0:
+            return lax.rem(zc + k, 4), yc
+        return zc, lax.rem(yc + k, 4)
+
+    def v_copy(hop, side, k):
+        axis = side if hop == 0 else 1 - side
+        to_z, to_y = v_peer(axis, k)
+        cols = slice(1024 * side, 1024 * side + 1024)
+        if hop == 0:
+            block = vfull.at[zc, yc, core, :, cols]
+        elif side == 0:
+            block = vfull.at[:, yc, core, :, cols]
+        else:
+            block = vfull.at[zc, :, core, :, cols]
+        return pltpu.make_async_remote_copy(
+            src_ref=block, dst_ref=block, send_sem=v_send.at[hop, side, k],
+            recv_sem=v_recv.at[hop, side, zc if axis == 0 else yc],
+            device_id={"rep": to_z * 8 + to_y * 2 + core}, device_id_type=MESH,
+        )
+
+    def v_wait(hop, side, k):
+        axis = side if hop == 0 else 1 - side
+        from_z, from_y = v_peer(axis, k)
+        cols = slice(1024 * side, 1024 * side + 1024)
+        if hop == 0:
+            block = vfull.at[from_z, from_y, core, :, cols]
+        elif side == 0:
+            block = vfull.at[:, from_y, core, :, cols]
+        else:
+            block = vfull.at[from_z, :, core, :, cols]
+        pltpu.make_async_remote_copy(
+            src_ref=block, dst_ref=block, send_sem=v_send.at[hop, side, k],
+            recv_sem=v_recv.at[hop, side, from_z if axis == 0 else from_y],
+            device_id={"rep": from_z * 8 + from_y * 2 + core}, device_id_type=MESH,
+        ).wait_recv()
+
+    def v_start(hop):
+        for side in range(2):
+            for k in (2, 1, 3):
+                v_copy(hop, side, k).start()
+
+    def v_wait_all(hop):
+        for side in range(2):
+            for k in (1, 3, 2):
+                v_wait(hop, side, k)
+
+    v_start(0)
+
     rope_copy.wait()
 
-    def rope_step(n, _):
-        a, b = n // 4, lax.rem(n, 4)
+    def rope_step(a, _):
         top = pl.multiple_of(a * 32, 32)
         cat = jnp.concatenate(
             [
@@ -176,84 +291,16 @@
             ],
             axis=0,
         )
-        got = jnp.dot(pick[pl.ds(pl.multiple_of(b * 256, 256), 256), :], cat, preferred_element_type=F32)
         keep = (iota((256, 128), 1) < DR) == (lax.rem(iota((256, 128), 0), 2) == 0)
-        for g in range(2):
-            v = got[:, 128 * g : 128 * g + 128]
-            v = jnp.where(keep, v, pltpu.roll(v, DR, 1)).astype(BF16)
-            zpool[pl.ds(a * 32 + g * 16 + b * 4, 4)] = v.reshape(4, 64, 128)
-        return 0
-
-    lax.fori_loop(0, 40, rope_step, 0)
-
-    for n in range(2):
-        own_copy(n).wait()
-        for k in range(1, XN):
-            a_wait(n, k)
-    for k in range(XN):
-        wf[12 * k : 12 * k + 12, :] = wx[k].astype(F32)
-        kf[4 * k : 4 * k + 4, :] = kx[k].astype(F32)
-    low48 = iota((48, 128), 1) < DR
-    low24 = iota((24, 128), 1) < DR
-    for p in range(HEADS // 2):
-        first = wf[:, 384 * p : 384 * p + 128]
-        mid = wf[:, 384 * p + 128 : 384 * p + 256]
-        last = wf[:, 384 * p + 256 : 384 * p + 384]
-        mid_r = pltpu.roll(mid, DR, 1)
-        last_r = pltpu.roll(last, DR, 1)
-        msend[2 * p, 0:48] = first.astype(BF16)
-        msend[2 * p + 1, 0:48] = jnp.where(low48, mid_r, last_r).astype(BF16)
-        pad = jnp.zeros((8, 128), F32)
-        even = jnp.concatenate([jnp.where(low24, mid[:24], mid_r[24:]), pad], axis=0)
-        odd = jnp.concatenate([jnp.where(low24, last_r[:24], last[24:]), pad], axis=0)
-        msend[2 * p, 64:96] = even.astype(BF16)
-        msend[2 * p + 1, 64:96] = odd.astype(BF16)
-        for g in range(2):
-            h = 2 * p + g
-            msend[h, 48:64] = kf[:, 128 * h : 128 * h + 128].astype(BF16)
-
-    def m_copy(k):
-        to = lax.rem(r + k, REP)
-        return pltpu.make_async_remote_copy(
-            src_ref=msend.at[lax.rem(to, GROUP)], dst_ref=mrecv.at[r], send_sem=m_send.at[k], recv_sem=m_recv.at[r],
-            device_id={"rep": to}, device_id_type=MESH,
-        )
-
-    def m_start(k, _):
-        m_copy(k).start()
-        return 0
-
-    lax.fori_loop(1, REP, m_start, 0)
-    mrecv[r] = msend[mine]
-
-    def x_wait(k, _):
-        frm = lax.rem(cell + k, 8)
-        pltpu.make_async_remote_copy(
-            src_ref=xsend, dst_ref=xrecv.at[frm, core], send_sem=x_send.at[k], recv_sem=x_recv.at[frm],
-            device_id={"rep": base + 2 * frm + core}, device_id_type=MESH,
-        ).wait_recv()
-        return 0
-
-    lax.fori_loop(1, 8, x_wait, 0)
-    xc = pltpu.make_async_remote_copy(
-        src_ref=xrecv.at[:, core], dst_ref=xrecv.at[:, core], send_sem=xc_sem.at[0], recv_sem=xc_sem.at[1],
-        device_id={"rep": other}, device_id_type=MESH,
-    )
-    xc.start()
-
-    own_copy(2).wait()
-    for k in range(1, XN):
-        a_wait(2, k)
-    for k in range(XN):
-        kf[4 * k : 4 * k + 4, :] = vx[k].astype(F32)
-    vfull[chip, core] = kf[...].astype(BF16)
-
-    def v_copy(k):
-        to = lax.rem(chip + k, 16)
-        return pltpu.make_async_remote_copy(
-            src_ref=vfull.at[chip, core], dst_ref=vfull.at[chip, core], send_sem=v_send.at[k], recv_sem=v_recv.at[chip],
-            device_id={"rep": 2 * to + core}, device_id_type=MESH,
-        )
+        for b in range(4):
+            got = jnp.dot(pick[256 * b : 256 * b + 256, :], cat, preferred_element_type=F32)
+            for g in range(2):
+                v = got[:, 128 * g : 128 * g + 128]
+                v = jnp.where(keep, v, pltpu.roll(v, DR, 1)).astype(BF16)
+                zpool[pl.ds(a * 32 + g * 16 + b * 4, 4)] = v.reshape(4, 64, 128)
+        return 0
+
+    lax.fori_loop(0, POOL // 32, rope_step, 0)
 
     pltpu.make_async_remote_copy(
         src_ref=xrecv.at[:, 1 - core], dst_ref=xrecv.at[:, 1 - core], send_sem=xc_sem.at[0], recv_sem=xc_sem.at[1],
@@ -293,54 +340,54 @@
 
     lax.fori_loop(0, REP, place, 0)
 
-    raw = jnp.dot(xexp[...].reshape(GROUP * 32, QR), wall[...], preferred_element_type=F32).reshape(GROUP, 32, 256)
-    tail = raw[:, 16:24] + raw[:, 24:32]
-    tail = tail + jnp.concatenate([tail[:, 4:8], tail[:, 0:4]], axis=1)
-    main = raw[:, 0:16].reshape(GROUP * 16, 256)
-    tail = tail.reshape(GROUP * 8, 256)
-    both = jnp.concatenate([main, tail], axis=0)
-    nope = both[:, :128]
-    hi = nope.astype(BF16)
-    lo = (nope - hi.astype(F32)).astype(BF16)
     key = mrecv[:, 48:64, :].reshape(LAT, 128)
-    lat = lax.dot_general(
-        jnp.concatenate([hi, lo], axis=1), jnp.concatenate([key, key], axis=1), NT, preferred_element_type=F32
-    )
-    rot = both[:, 128:]
-    rot_hi = rot.astype(BF16).astype(F32)
-    rot = jnp.where(iota(rot.shape, 1) < DR, rot_hi, rot - rot_hi)
-    nmain = GROUP * 16
-    qsend[:, :, 0:512] = lat[:nmain].astype(BF16).reshape(GROUP, 16, 512)
-    qsend[:, :, 512:640] = rot[:nmain].astype(BF16).reshape(GROUP, 16, 128)
-    ltail = lat[nmain:].reshape(GROUP, 8, 512)
-    upper = iota((GROUP, 8, 128), 1) < 4
-    pair = [
-        jnp.where(upper, ltail[:, :, 256 * n : 256 * n + 128], ltail[:, :, 256 * n + 128 : 256 * n + 256])
-        for n in range(2)
-    ]
-    qsend[:, :, 640:768] = jnp.concatenate(pair, axis=1).astype(BF16)
-    rtail = rot[nmain:].reshape(GROUP, 8, 128)
-    qsend[:, :, 768:896] = jnp.concatenate([rtail, rtail], axis=1).astype(BF16)
-
-    def q_copy(k):
-        to = lax.rem(mine + k, GROUP)
+    key = jnp.concatenate([key, key], axis=1)
+    half = GROUP // 2
+
+    def q_copy(to):
         return pltpu.make_async_remote_copy(
-            src_ref=qsend.at[to], dst_ref=qrecv.at[mine], send_sem=q_send.at[k], recv_sem=q_recv.at[mine],
+            src_ref=qsend.at[to], dst_ref=qrecv.at[mine], send_sem=q_send.at[to], recv_sem=q_recv.at[mine],
             device_id={"rep": base + to}, device_id_type=MESH,
         )
 
-    def q_start(k, _):
-        q_copy(k).start()
-        return 0
-
-    lax.fori_loop(1, GROUP, q_start, 0)
+    for e in (1, 0):
+        group = pl.multiple_of(lax.rem(mine // half + e, 2) * half, half)
+        members = pl.ds(group, half)
+        raw = jnp.dot(xexp[members].reshape(half * 32, QR), wall[...], preferred_element_type=F32)
+        raw = raw.reshape(half, 32, 256)
+        tail = raw[:, 16:24] + raw[:, 24:32]
+        tail = tail + jnp.concatenate([tail[:, 4:8], tail[:, 0:4]], axis=1)
+        both = jnp.concatenate([raw[:, 0:16].reshape(half * 16, 256), tail.reshape(half * 8, 256)], axis=0)
+        nope = both[:, :128]
+        hi = nope.astype(BF16)
+        lo = (nope - hi.astype(F32)).astype(BF16)
+        lat = lax.dot_general(jnp.concatenate([hi, lo], axis=1), key, NT, preferred_element_type=F32)
+        rot = both[:, 128:]
+        rot_hi = rot.astype(BF16).astype(F32)
+        rot = jnp.where(iota(rot.shape, 1) < DR, rot_hi, rot - rot_hi)
+        nmain = half * 16
+        qsend[members, :, 0:512] = lat[:nmain].astype(BF16).reshape(half, 16, 512)
+        qsend[members, :, 512:640] = rot[:nmain].astype(BF16).reshape(half, 16, 128)
+        ltail = lat[nmain:].reshape(half, 8, 512)
+        upper = iota((half, 8, 128), 1) < 4
+        pair = [
+            jnp.where(upper, ltail[:, :, 256 * n : 256 * n + 128], ltail[:, :, 256 * n + 128 : 256 * n + 256])
+            for n in range(2)
+        ]
+        qsend[members, :, 640:768] = jnp.concatenate(pair, axis=1).astype(BF16)
+        rtail = rot[nmain:].reshape(half, 8, 128)
+        qsend[members, :, 768:896] = jnp.concatenate([rtail, rtail], axis=1).astype(BF16)
+
+        def q_start(k, _, e=e, group=group):
+            q_copy(group + lax.rem(mine + k, half)).start()
+            return 0
+
+        lax.fori_loop(1 - e, half, q_start, 0)
+
     qrecv[mine] = qsend[mine]
 
-    def v_start(k, _):
-        v_copy(k).start()
-        return 0
-
-    lax.fori_loop(1, 16, v_start, 0)
+    v_wait_all(0)
+    v_start(1)
 
     perm_row = iota((256, 256), 0)
     want = lax.rem(perm_row // 4, 16) * 16 + (perm_row // 64) * 4 + lax.rem(perm_row, 4)
@@ -465,17 +512,9 @@
         att[i] = acc[...] * col
 
     def forward():
-        def v_wait(k, _):
-            frm = lax.rem(chip + k, 16)
-            pltpu.make_async_remote_copy(
-                src_ref=vfull.at[frm, core], dst_ref=vfull.at[frm, core], send_sem=v_send.at[k],
-                recv_sem=v_recv.at[frm], device_id={"rep": 2 * frm + core}, device_id_type=MESH,
-            ).wait_recv()
-            return 0
-
-        lax.fori_loop(1, 16, v_wait, 0)
+        v_wait_all(1)
         pltpu.make_async_remote_copy(
-            src_ref=vfull.at[:, core], dst_ref=vfull.at[:, core], send_sem=vc_sem.at[0], recv_sem=vc_sem.at[1],
+            src_ref=vfull.at[:, :, core], dst_ref=vfull.at[:, :, core], send_sem=vc_sem.at[0], recv_sem=vc_sem.at[1],
             device_id={"rep": other}, device_id_type=MESH,
         ).start()
 
@@ -488,32 +527,30 @@
             weigh_fresh(i - 1, bufs[(i - 1) % 2], (i - 1) % 2)
 
         def step(c, _, i=i):
-            if i < REQ:
-                scores(i, bufs[i % 2], i % 2)(c)
-            if i > 0:
-                weigh(i - 1, bufs[(i - 1) % 2], (i - 1) % 2)(c)
+            for d in range(UNROLL):
+                if i < REQ:
+                    scores(i, bufs[i % 2], i % 2)(c * UNROLL + d)
+                if i > 0:
+                    weigh(i - 1, bufs[(i - 1) % 2], (i - 1) % 2)(c * UNROLL + d)
             return 0
 
-        lax.fori_loop(0, 4, step, 0)
+        lax.fori_loop(0, 4 // UNROLL, step, 0)
         if i > 0:
             finish(i - 1)
         if i == 3:
             forward()
 
     pltpu.make_async_remote_copy(
-        src_ref=vfull.at[:, 1 - core], dst_ref=vfull.at[:, 1 - core], send_sem=vc_sem.at[0], recv_sem=vc_sem.at[1],
+        src_ref=vfull.at[:, :, 1 - core], dst_ref=vfull.at[:, :, 1 - core], send_sem=vc_sem.at[0], recv_sem=vc_sem.at[1],
         device_id={"rep": other}, device_id_type=MESH,
     ).wait_recv()
     for p in range(HEADS // 2):
         rows = att[:, 8 * p : 8 * p + 8, :].reshape(REQ * 8, LAT).astype(BF16)
-        v = vfull[:, :, :, 256 * p : 256 * p + 256].reshape(LAT, 256)
+        v = vfull[:, :, :, :, 256 * p : 256 * p + 256].reshape(LAT, 256)
         o = jnp.dot(rows, v, preferred_element_type=F32).reshape(REQ, 8, 256)
         for i in range(REQ):
-            for s in range(STEPS):
-                outf[s, i : i + 1, 256 * p : 256 * p + 128] = o[i, s : s + 1, 0:128]
-                outf[s, i : i + 1, 256 * p + 128 : 256 * p + 256] = o[i, 4 + s : 5 + s, 128:256]
-    for s in range(STEPS):
-        out_ref[s] = outf[s, 0:REQ].astype(BF16)
+            out_ref[i, :, 256 * p : 256 * p + 128] = o[i, 0:4, 0:128].astype(BF16)
+            out_ref[i, :, 256 * p + 128 : 256 * p + 256] = o[i, 4:8, 128:256].astype(BF16)
 
     for n in range(3):
         for k in range(1, XN):
@@ -527,19 +564,23 @@
     xc.wait_send()
 
     def drain_m(k, _):
-        m_copy(k).wait_send()
+        to = lax.rem(r + k, REP)
+        m_copy(lax.rem(to, GROUP), to // GROUP)[1].wait_send()
         return 0
 
     lax.fori_loop(1, REP, drain_m, 0)
 
-    def drain_qv(k, _):
-        q_copy(k).wait_send()
-        v_copy(k).wait_send()
-        return 0
-
-    lax.fori_loop(1, 16, drain_qv, 0)
+    def drain_q(k, _):
+        q_copy(lax.rem(mine + k, GROUP)).wait_send()
+        return 0
+
+    lax.fori_loop(1, GROUP, drain_q, 0)
+    for hop in range(2):
+        for side in range(2):
+            for k in range(1, 4):
+                v_copy(hop, side, k).wait_send()
     pltpu.make_async_remote_copy(
-        src_ref=vfull.at[:, core], dst_ref=vfull.at[:, core], send_sem=vc_sem.at[0], recv_sem=vc_sem.at[1],
+        src_ref=vfull.at[:, :, core], dst_ref=vfull.at[:, :, core], send_sem=vc_sem.at[0], recv_sem=vc_sem.at[1],
         device_id={"rep": other}, device_id_type=MESH,
     ).wait_send()
 
@@ -552,9 +593,9 @@
     smem = pl.BlockSpec(memory_space=pltpu.SMEM)
     hbm = pl.BlockSpec(memory_space=pl.ANY)
     dma = pltpu.SemaphoreType.DMA
-    return pl.pallas_call(
+    out = pl.pallas_call(
         kernel,
-        out_shape=jax.ShapeDtypeStruct((STEPS, REQ, HEADS * DN), BF16),
+        out_shape=jax.ShapeDtypeStruct((REQ, STEPS, HEADS * DN), BF16),
         in_specs=[vmem, vmem, hbm, hbm, smem, smem, smem, hbm, hbm, hbm, vmem],
         out_specs=vmem,
         scratch_shapes=[
@@ -568,7 +609,7 @@
             pltpu.VMEM((16, 2048), F32),
             pltpu.VMEM((HEADS, MSG, 128), BF16),
             pltpu.VMEM((REP, MSG, 128), BF16),
-            pltpu.VMEM((16, 2, 16, 2048), BF16),
+            pltpu.VMEM((4, 4, 2, 16, 2048), BF16),
             pltpu.VMEM((16, XW), F32),
             pltpu.VMEM((16, XW), BF16),
             pltpu.VMEM((8, 2, 16, XW), BF16),
@@ -586,17 +627,17 @@
             pltpu.VMEM((REQ, 8, 640), F32),
             pltpu.VMEM((REQ, 2, 8, 128), F32),
             pltpu.VMEM((1024, 512), BF16),
-            pltpu.VMEM((STEPS, 8, HEADS * DN), F32),
             pltpu.SMEM((REP,), jnp.int32),
             dma((2,)), dma((3,)), dma((3, XN)), dma((3, XN)),
             dma((8,)), dma((8,)), dma((2,)), dma((REP,)), dma((REP,)),
-            dma((16,)), dma((16,)), dma((2,)), dma((GROUP,)), dma((GROUP,)),
+            dma((2, 2, 4)), dma((2, 2, 4)), dma((2,)), dma((GROUP,)), dma((GROUP,)),
         ],
         compiler_params=pltpu.CompilerParams(
             collective_id=0, has_side_effects=True, vmem_limit_bytes=60 * 2**20
         ),
         name="latent_attention",
-    )(query_latent, new_entry, cache_latent, cache_rope, block_table, context_len, owner_rows, query_up, key_up, value_up, freq)
+    )(jnp.swapaxes(query_latent, 0, 1), jnp.swapaxes(new_entry, 0, 1), cache_latent, cache_rope, block_table, context_len, owner_rows, query_up, key_up, value_up, freq)
+    return jnp.swapaxes(out, 0, 1)
 
 
 def solution(mesh):

time: 72.5 us -> 61 us (0.84)
  Pallas kernels: 67.8 us -> 59.2 us
  local copies, waits for them, and re-layouts: 4.46 us -> 1.55 us
    pallas_call x1, Pallas kernels: 67.8 us -> 59.2 us  [on_device(): pl.pallas_call(kernel, out_shape=jax.ShapeDtypeStruct((REQ, STEPS, HEADS...]
    pallas_call x1 -> x0, local copies, waits for them, and re-layouts: 1.61 us -> none  [on_device(): pl.pallas_call(kernel, out_shape=jax.ShapeDtypeStruct((STEPS, REQ, HEADS...]
    unnamed x2 -> x1, local copies, waits for them, and re-layouts: 2.84 us -> 1.55 us
where the time goes in v2:
time: 61 us; the launch traced here: 60.8 us
  Pallas kernels  59.2 us (97%)
  local copies, waits for them, and re-layouts  1.55 us (3%)
    pallas_call x1, Pallas kernels, on_device(): pl.pallas_call(kernel, out_shape=jax.ShapeDtypeStruct((REQ, STEPS, HEADS...  59.2 us
    unnamed x1, local copies, waits for them, and re-layouts  1.55 us

profile of v2, /device:TPU:1, one launch (start us, length us, event | category | flops | bytes accessed | tf_op | source)
XLA Modules:
  0.0 60.8 jit_solution(17923784344835669598)
XLA Ops:
  0.0 59.2 %latent_attention.1 = bf16[5,4,2048]{2,1,0:T(4,128)(2,1)} custom-call(bf16[5,4,1536]{2,1,0:T(4,128)(2,1)} %bitcast.4, bf16[5,4,576]{2,1,0:T(4,128)(2,1)} %bitcast.5, bf16[320,64,512]{2,1,0:T(8,128)(2,1)} %lat_hbm.1, bf16[320,4096]{1,0:T(8,128)(2,1)} %rope_hbm.1, s32[5,64]{1,0:T(8,128)} %bt.1, s32[5]{0:T(128)} %ln.1, s32[32]{0:T(128)} %own.1, ...), custom_call_target="tpu_custom_call" | custom-call | tf_op jit(solution)/shard_map/latent_attention/pallas_call | solution.py:596
  59.2 1.6 %copy.13 = bf16[4,5,2048]{2,0,1:T(4,128)(2,1)} copy(bf16[4,5,2048]{2,0,1:T(4,128)(2,1)} %bitcast.3) | data formatting | bytes 163840

commit v3 on v2

--- a/solution.py
+++ b/solution.py
@@ -22,10 +22,9 @@
 TAIL = QR // 4
 XW = QR + TAIL
 MSG = 96
-QW = 896
 SCALE = float((DN + DR) ** -0.5 * np.log2(np.e))
 NEG = -1e30
-UNROLL = 2
+GATHER = 2
 MESH = pl.DeviceIdType.MESH
 F32 = jnp.float32
 BF16 = jnp.bfloat16
@@ -39,9 +38,9 @@
 def kernel(
     x_ref, ne_ref, lat_hbm, rope_hbm, bt, ln, own, wq_hbm, wk_hbm, wv_hbm, freq_ref, out_ref,
     pool, zpool, rope, wx, kx, vx, wf, kf, msend, mrecv, vfull, xs, xsend, xrecv, xexp, wall,
-    qsend, qrecv, wqt, s_a, s_b, m_sc, l_sc, acc, att, nef, cs, pick, inv,
+    qsend, qrecv, qsend2, qrecv2, wqt, s_a, s_b, m_sc, l_sc, acc, att, nef, cs, pick, inv,
     sem_local, sem_own, a_send, a_recv, x_send, x_recv, xc_sem, m_send, m_recv,
-    v_send, v_recv, vc_sem, q_send, q_recv,
+    v_send, v_recv, vc_sem, q_send, q_recv, row_sem, plane_sem,
 ):
     r = lax.axis_index("rep")
     hx = lax.axis_index("head")
@@ -51,6 +50,7 @@
     base = (r // GROUP) * GROUP
     mine = lax.rem(r, GROUP)
     cell = mine // 2
+    head = core * 8 + cell
     other = r + 1 - 2 * core
 
     rope_copy = pltpu.make_async_copy(rope_hbm, rope, sem_local.at[0])
@@ -58,15 +58,65 @@
     pool_copy = pltpu.make_async_copy(lat_hbm, pool, sem_local.at[1])
     pool_copy.start()
 
+    def along(axis, k):
+        if axis == "x":
+            return {"head": lax.rem(hx + k, XN)}
+        if axis == "core":
+            return {"rep": other}
+        if axis == "y":
+            return {"rep": zc * 8 + lax.rem(yc + k, 4) * 2 + core}
+        return {"rep": lax.rem(zc + k, 4) * 8 + yc * 2 + core}
+
     barrier = pltpu.get_barrier_semaphore()
-    for k in range(1, XN):
-        pl.semaphore_signal(barrier, inc=1, device_id={"head": lax.rem(hx + k, XN)}, device_id_type=MESH)
-
-    def greet(k, _):
-        pl.semaphore_signal(barrier, inc=1, device_id={"rep": lax.rem(r + k, REP)}, device_id_type=MESH)
-        return 0
-
-    lax.fori_loop(1, REP, greet, 0)
+    for axis in ("x", "core", "y", "z"):
+        for k in range(1, 2 if axis == "core" else 4):
+            pl.semaphore_signal(barrier, inc=1, device_id=along(axis, k), device_id_type=MESH)
+
+    pl.semaphore_wait(barrier, 10)
+
+    parts = (
+        (wk_hbm, kx, 2048, 0, 2048),
+        (wq_hbm, wx, 3072, 0, 1536),
+        (wq_hbm, wx, 3072, 1536, 1536),
+        (wv_hbm, vx, 2048, 0, 2048),
+    )
+
+    def a_source(n, to):
+        src, dst, width, first, size = parts[n]
+        return src.at[:, pl.ds(pl.multiple_of(to * width + first, 128), size)]
+
+    def a_block(n, frm):
+        src, dst, width, first, size = parts[n]
+        return dst.at[frm, :, first : first + size]
+
+    def a_copy(n, k):
+        to = lax.rem(hx + k, XN)
+        return pltpu.make_async_remote_copy(
+            src_ref=a_source(n, to), dst_ref=a_block(n, hx), send_sem=a_send.at[n, k], recv_sem=a_recv.at[n, hx],
+            device_id={"head": to}, device_id_type=MESH,
+        )
+
+    def a_wait(n):
+        own_copy(n).wait()
+        for k in range(1, XN):
+            frm = lax.rem(hx + k, XN)
+            pltpu.make_async_remote_copy(
+                src_ref=a_block(n, frm), dst_ref=a_block(n, frm), send_sem=a_send.at[n, k], recv_sem=a_recv.at[n, frm],
+                device_id={"head": frm}, device_id_type=MESH,
+            ).wait_recv()
+
+    def own_copy(n):
+        return pltpu.make_async_copy(a_source(n, hx), a_block(n, hx), sem_own.at[n])
+
+    def a_start(n):
+        for k in (2, 1, 3):
+            a_copy(n, k).start()
+        own_copy(n).start()
+
+    for n in range(3):
+        a_start(n)
+    for k in range(1, 4):
+        pl.semaphore_signal(row_sem, inc=1, device_id=along("y", k), device_id_type=MESH)
 
     for i in range(4):
         xs[4 * i : 4 * i + 4, :QR] = x_ref[i].astype(F32)
@@ -75,40 +125,20 @@
         xs[4 * j : 4 * j + 4, QR:] = row[:, TAIL * j : TAIL * (j + 1)]
     xsend[...] = xs[...].astype(BF16)
 
-    pl.semaphore_wait(barrier, XN - 1 + REP - 1)
-
-    parts = ((wq_hbm, wx, 3072), (wk_hbm, kx, 2048), (wv_hbm, vx, 2048))
-
-    def a_copy(n, k):
-        src, dst, width = parts[n]
-        to = lax.rem(hx + k, XN)
-        return pltpu.make_async_remote_copy(
-            src_ref=src.at[:, pl.ds(pl.multiple_of(to * width, 128), width)],
-            dst_ref=dst.at[hx],
-            send_sem=a_send.at[n, k],
-            recv_sem=a_recv.at[n, hx],
-            device_id={"head": to},
-            device_id_type=MESH,
-        )
-
-    def a_wait(n, k):
-        src, dst, width = parts[n]
-        frm = lax.rem(hx + k, XN)
-        pltpu.make_async_remote_copy(
-            src_ref=dst.at[frm], dst_ref=dst.at[frm], send_sem=a_send.at[n, k], recv_sem=a_recv.at[n, frm],
-            device_id={"head": frm}, device_id_type=MESH,
-        ).wait_recv()
-
-    def own_copy(n):
-        src, dst, width = parts[n]
-        return pltpu.make_async_copy(
-            src.at[:, pl.ds(pl.multiple_of(hx * width, 128), width)], dst.at[hx], sem_own.at[n]
-        )
-
-    for n in range(3):
-        for k in (2, 1, 3):
-            a_copy(n, k).start()
-        own_copy(n).start()
+    pl.semaphore_wait(row_sem, 3)
+    for k in range(1, 4):
+        pl.semaphore_signal(plane_sem, inc=1, device_id=along("z", k), device_id_type=MESH)
+
+    def invert(j, _):
+        at = jnp.int32(0)
+        for n in range(REP):
+            at = jnp.where(own[n] == j, jnp.int32(n), at)
+        inv[j] = at
+        return 0
+
+    lax.fori_loop(0, REP, invert, 0)
+
+    pl.semaphore_wait(plane_sem, 3)
 
     def x_copy(k):
         to = lax.rem(cell + k, 8)
@@ -123,15 +153,6 @@
 
     lax.fori_loop(1, 8, x_start, 0)
     xrecv[cell, core] = xsend[...]
-
-    def invert(j, _):
-        at = jnp.int32(0)
-        for n in range(REP):
-            at = jnp.where(own[n] == j, jnp.int32(n), at)
-        inv[j] = at
-        return 0
-
-    lax.fori_loop(0, REP, invert, 0)
 
     lane8 = iota((8, 128), 1)
     sub8 = iota((8, 128), 0)
@@ -159,25 +180,21 @@
         (pcol // 16 == lax.rem(prow, 64) // 2) & (lax.rem(pcol, 16) == prow // 64), 1.0, 0.0
     ).astype(BF16)
 
-    for n in range(2):
-        own_copy(n).wait()
-        for k in range(1, XN):
-            a_wait(n, k)
+    a_wait(0)
     for k in range(XN):
-        wf[12 * k : 12 * k + 12, :] = wx[k].astype(F32)
         kf[4 * k : 4 * k + 4, :] = kx[k].astype(F32)
     low48 = iota((48, 128), 1) < DR
     low24 = iota((24, 128), 1) < DR
 
     def m_copy(h, half):
-        to = half * GROUP + h
+        to = half * GROUP + lax.rem(h, 8) * 2 + h // 8
         return to, pltpu.make_async_remote_copy(
             src_ref=msend.at[h], dst_ref=mrecv.at[r], send_sem=m_send.at[to], recv_sem=m_recv.at[r],
             device_id={"rep": to}, device_id_type=MESH,
         )
 
-    def make(k, _):
-        p = lax.rem(cell + k, HEADS // 2)
+    def make(n, k):
+        p = n * 4 + lax.rem(cell // 2 + k, 4)
         col = pl.multiple_of(p * 384, 128)
         first = wf[:, pl.ds(col, 128)]
         mid = wf[:, pl.ds(pl.multiple_of(col + 128, 128), 128)]
@@ -193,18 +210,29 @@
         msend[2 * p + 1, 0:48] = jnp.where(low48, mid_r, last_r).astype(BF16)
         msend[2 * p + 1, 48:64] = kf[:, pl.ds(pl.multiple_of(p * 256 + 128, 128), 128)].astype(BF16)
         msend[2 * p + 1, 64:96] = odd.astype(BF16)
-        for g in range(2):
-            for half in range(2):
+        for half in range(2):
+            for g in range(2):
                 to, copy = m_copy(2 * p + g, half)
 
                 @pl.when(to != r)
                 def _(copy=copy):
                     copy.start()
 
-        return 0
-
-    lax.fori_loop(0, HEADS // 2, make, 0)
-    mrecv[r] = msend[mine]
+    def make_half(n):
+        a_wait(1 + n)
+        for k in range(XN):
+            wf[12 * k : 12 * k + 12, 1536 * n : 1536 * n + 1536] = wx[k, :, 1536 * n : 1536 * n + 1536].astype(F32)
+
+        def one(k, _):
+            make(n, k)
+            return 0
+
+        lax.fori_loop(0, 4, one, 0)
+
+    make_half(0)
+    make_half(1)
+    a_start(3)
+    mrecv[r] = msend[head]
 
     def x_wait(k, _):
         frm = lax.rem(cell + k, 8)
@@ -221,9 +249,7 @@
     )
     xc.start()
 
-    own_copy(2).wait()
-    for k in range(1, XN):
-        a_wait(2, k)
+    a_wait(3)
     for k in range(XN):
         kf[4 * k : 4 * k + 4, :] = vx[k].astype(F32)
     vfull[zc, yc, core] = kf[...].astype(BF16)
@@ -344,9 +370,12 @@
     key = jnp.concatenate([key, key], axis=1)
     half = GROUP // 2
 
-    def q_copy(to):
+    qparts = ((qsend, qrecv), (qsend2, qrecv2))
+
+    def q_copy(n, to):
+        src, dst = qparts[n]
         return pltpu.make_async_remote_copy(
-            src_ref=qsend.at[to], dst_ref=qrecv.at[mine], send_sem=q_send.at[to], recv_sem=q_recv.at[mine],
+            src_ref=src.at[to], dst_ref=dst.at[head], send_sem=q_send.at[n, to], recv_sem=q_recv.at[n, mine],
             device_id={"rep": base + to}, device_id_type=MESH,
         )
 
@@ -366,25 +395,37 @@
         rot_hi = rot.astype(BF16).astype(F32)
         rot = jnp.where(iota(rot.shape, 1) < DR, rot_hi, rot - rot_hi)
         nmain = half * 16
-        qsend[members, :, 0:512] = lat[:nmain].astype(BF16).reshape(half, 16, 512)
-        qsend[members, :, 512:640] = rot[:nmain].astype(BF16).reshape(half, 16, 128)
+        lmain = lat[:nmain].reshape(half, 16, 512)
+        rmain = rot[:nmain].reshape(half, 16, 128)
         ltail = lat[nmain:].reshape(half, 8, 512)
+        rtail = rot[nmain:].reshape(half, 8, 128)
+        first = lmain[:, 0:8]
+        qsend[members, :, 0:256] = jnp.concatenate([first[:, :, :256], first[:, :, 256:]], axis=1).astype(BF16)
+        qsend[members, :, 256:384] = jnp.concatenate([rmain[:, 0:8], rmain[:, 0:8]], axis=1).astype(BF16)
+
+        def q_start(k, _, e=e, group=group):
+            q_copy(0, group + lax.rem(mine + k, half)).start()
+            return 0
+
+        lax.fori_loop(1 - e, half, q_start, 0)
+        second = lmain[:, 8:16]
+        qsend2[members, :, 0:256] = jnp.concatenate([second[:, :, :256], second[:, :, 256:]], axis=1).astype(BF16)
+        qsend2[members, :, 256:384] = jnp.concatenate([rmain[:, 8:16], rtail], axis=1).astype(BF16)
         upper = iota((half, 8, 128), 1) < 4
         pair = [
             jnp.where(upper, ltail[:, :, 256 * n : 256 * n + 128], ltail[:, :, 256 * n + 128 : 256 * n + 256])
             for n in range(2)
         ]
-        qsend[members, :, 640:768] = jnp.concatenate(pair, axis=1).astype(BF16)
-        rtail = rot[nmain:].reshape(half, 8, 128)
-        qsend[members, :, 768:896] = jnp.concatenate([rtail, rtail], axis=1).astype(BF16)
-
-        def q_start(k, _, e=e, group=group):
-            q_copy(group + lax.rem(mine + k, half)).start()
-            return 0
-
-        lax.fori_loop(1 - e, half, q_start, 0)
-
-    qrecv[mine] = qsend[mine]
+        qsend2[members, :, 384:512] = jnp.concatenate(pair, axis=1).astype(BF16)
+
+    def q_start2(k, _):
+        q_copy(1, lax.rem(mine + half + k, GROUP)).start()
+        return 0
+
+    lax.fori_loop(0, half, q_start2, 0)
+    lax.fori_loop(half + 1, GROUP, q_start2, 0)
+    qrecv[head] = qsend[mine]
+    qrecv2[head] = qsend2[mine]
 
     v_wait_all(0)
     v_start(1)
@@ -393,26 +434,24 @@
     want = lax.rem(perm_row // 4, 16) * 16 + (perm_row // 64) * 4 + lax.rem(perm_row, 4)
     perm = jnp.where(iota((256, 256), 1) == want, 1.0, 0.0).astype(BF16)
 
-    def q_wait(k, _):
-        frm = lax.rem(mine + k, GROUP)
-        pltpu.make_async_remote_copy(
-            src_ref=qsend.at[frm], dst_ref=qrecv.at[frm], send_sem=q_send.at[k], recv_sem=q_recv.at[frm],
-            device_id={"rep": base + frm}, device_id_type=MESH,
-        ).wait_recv()
-        return 0
-
-    lax.fori_loop(1, GROUP, q_wait, 0)
+    def q_wait_all(n):
+        src, dst = qparts[n]
+
+        def q_wait(k, _):
+            frm = lax.rem(mine + k, GROUP)
+            slot = lax.rem(frm, 2) * 8 + frm // 2
+            pltpu.make_async_remote_copy(
+                src_ref=src.at[frm], dst_ref=dst.at[slot], send_sem=q_send.at[n, frm], recv_sem=q_recv.at[n, frm],
+                device_id={"rep": base + frm}, device_id_type=MESH,
+            ).wait_recv()
+            return 0
+
+        lax.fori_loop(1, GROUP, q_wait, 0)
 
     low_q = iota((LAT, 128), 1) < DR
     low_r = iota((DR, 128), 1) < DR
-    got = jnp.dot(perm, qrecv[...].reshape(GROUP * 16, QW), preferred_element_type=F32)
-    for i in range(REQ):
-        if i < 4:
-            lat_i = got[64 * i : 64 * i + 64, :512]
-            rp = got[64 * i : 64 * i + 64, 512:640]
-        else:
-            lat_i = jnp.concatenate([got[64 * j : 64 * j + 64, 640:768] for j in range(4)], axis=1)
-            rp = got[0:64, 768:896]
+
+    def stationary(i, lat_i, rp):
         rr = rp + pltpu.roll(rp, DR, 1)
         cos = jnp.concatenate([cs[i, 0]] * 8, axis=0)
         sin = jnp.concatenate([cs[i, 1]] * 8, axis=0)
@@ -432,6 +471,19 @@
         wqt[i, 2176:2240, 128:256] = rleft
         wqt[i, 2240:2304, 128:256] = rright
 
+    def queries(n):
+        q_wait_all(n)
+        dst = qparts[n][1]
+        got = jnp.dot(perm, dst[...].reshape(GROUP * 16, dst.shape[2]), preferred_element_type=F32)
+        for m in range(2):
+            left = got[64 * m : 64 * m + 64, :256]
+            right = got[128 + 64 * m : 192 + 64 * m, :256]
+            stationary(2 * n + m, jnp.concatenate([left, right], axis=1), got[64 * m : 64 * m + 64, 256:384])
+        if n == 1:
+            lat_i = jnp.concatenate([got[64 * j : 64 * j + 64, 384:512] for j in range(4)], axis=1)
+            stationary(4, lat_i, got[128:192, 256:384])
+
+    queries(0)
     pool_copy.wait()
 
     def page(i, c, k, g):
@@ -440,30 +492,32 @@
     def keys(i, c, k):
         return jnp.concatenate([pool[page(i, c, k, g)] for g in range(4)], axis=0)
 
-    def scores(i, buf, slot):
-        def chunk(c):
-            s = jnp.dot(keys(i, c, 0), wqt[i, 0:512], preferred_element_type=F32)
-            for k in range(1, 4):
-                s = s + jnp.dot(keys(i, c, k), wqt[i, 512 * k : 512 * k + 512], preferred_element_type=F32)
-            low = iota((64, 128), 1) < DR
-            rows = []
-            for g in range(4):
-                rows.append(
-                    jnp.concatenate(
-                        [
-                            jnp.where(low, zpool[page(i, c, 2 * e, g)], zpool[page(i, c, 2 * e + 1, g)])
-                            for e in range(2)
-                        ],
-                        axis=1,
-                    )
-                )
-            s = s + jnp.dot(jnp.concatenate(rows, axis=0), wqt[i, 2048:2304], preferred_element_type=F32)
-            token = iota((256, 256), 0) + (iota((256, 256), 1) // 64) * 256
-            s = jnp.where(token < ln[i] - c * 1024, s, NEG)
-            buf[pl.ds(pl.multiple_of(c * 256, 256), 256), :] = s
-            m_sc[slot] = jnp.maximum(m_sc[slot], jnp.max(s.reshape(32, 8, 256), axis=0))
-
-        return chunk
+    def scores(i, buf, slot, chunks):
+        size = 256 * len(chunks)
+        low = iota((64, 128), 1) < DR
+
+        def latents(k):
+            return jnp.concatenate([pool[page(i, c, k, g)] for c in chunks for g in range(4)], axis=0)
+
+        def rotary(e):
+            return jnp.concatenate(
+                [
+                    jnp.where(low, zpool[page(i, c, 2 * e, g)], zpool[page(i, c, 2 * e + 1, g)])
+                    for c in chunks
+                    for g in range(4)
+                ],
+                axis=0,
+            )
+
+        lhs = jnp.concatenate([latents(k) for k in range(4)] + [rotary(0), rotary(1)], axis=1)
+        s = jnp.dot(lhs, wqt[i], preferred_element_type=F32)
+        token = iota((256, 256), 0) + (iota((256, 256), 1) // 64) * 256
+        m = m_sc[slot]
+        for n, c in enumerate(chunks):
+            part = jnp.where(token < ln[i] - c * 1024, s[256 * n : 256 * n + 256], NEG)
+            buf[256 * c : 256 * c + 256, :] = part
+            m = jnp.maximum(m, jnp.max(part.reshape(32, 8, 256), axis=0))
+        m_sc[slot] = m
 
     def fresh(i, buf, slot):
         new = jnp.concatenate([nef[i], jnp.zeros((8, 640), F32)], axis=0).astype(BF16)
@@ -484,7 +538,7 @@
 
     def weigh(i, buf, slot):
         def chunk(c):
-            s = buf[pl.ds(pl.multiple_of(c * 256, 256), 256), :]
+            s = buf[256 * c : 256 * c + 256, :]
             p = jnp.exp2((s - m_sc[slot][0:1]) * SCALE)
             l_sc[...] = l_sc[...] + jnp.sum(p.reshape(32, 8, 256), axis=0)
             pt = jnp.transpose(p).astype(BF16)
@@ -520,21 +574,20 @@
 
     bufs = (s_a, s_b)
     for i in range(REQ + 1):
+        if i == 2:
+            queries(1)
         if i < REQ:
             fresh(i, bufs[i % 2], i % 2)
         if i > 0:
             m_sc[(i - 1) % 2] = top((i - 1) % 2)
             weigh_fresh(i - 1, bufs[(i - 1) % 2], (i - 1) % 2)
 
-        def step(c, _, i=i):
-            for d in range(UNROLL):
-                if i < REQ:
-                    scores(i, bufs[i % 2], i % 2)(c * UNROLL + d)
-                if i > 0:
-                    weigh(i - 1, bufs[(i - 1) % 2], (i - 1) % 2)(c * UNROLL + d)
-            return 0
-
-        lax.fori_loop(0, 4 // UNROLL, step, 0)
+        for c in range(0, 4, GATHER):
+            if i < REQ:
+                scores(i, bufs[i % 2], i % 2, list(range(c, c + GATHER)))
+            if i > 0:
+                for d in range(c, c + GATHER):
+                    weigh(i - 1, bufs[(i - 1) % 2], (i - 1) % 2)(d)
         if i > 0:
             finish(i - 1)
         if i == 3:
@@ -552,7 +605,7 @@
             out_ref[i, :, 256 * p : 256 * p + 128] = o[i, 0:4, 0:128].astype(BF16)
             out_ref[i, :, 256 * p + 128 : 256 * p + 256] = o[i, 4:8, 128:256].astype(BF16)
 
-    for n in range(3):
+    for n in range(4):
         for k in range(1, XN):
             a_copy(n, k).wait_send()
 
@@ -565,13 +618,14 @@
 
     def drain_m(k, _):
         to = lax.rem(r + k, REP)
-        m_copy(lax.rem(to, GROUP), to // GROUP)[1].wait_send()
+        m_copy(lax.rem(to, GROUP) // 2 + 8 * lax.rem(to, 2), to // GROUP)[1].wait_send()
         return 0
 
     lax.fori_loop(1, REP, drain_m, 0)
 
     def drain_q(k, _):
-        q_copy(lax.rem(mine + k, GROUP)).wait_send()
+        q_copy(0, lax.rem(mine + k, GROUP)).wait_send()
+        q_copy(1, lax.rem(mine + k, GROUP)).wait_send()
         return 0
 
     lax.fori_loop(1, GROUP, drain_q, 0)
@@ -615,8 +669,10 @@
             pltpu.VMEM((8, 2, 16, XW), BF16),
             pltpu.VMEM((GROUP, 32, QR), BF16),
             pltpu.VMEM((QR, 256), BF16),
-            pltpu.VMEM((GROUP, 16, QW), BF16),
-            pltpu.VMEM((GROUP, 16, QW), BF16),
+            pltpu.VMEM((GROUP, 16, 384), BF16),
+            pltpu.VMEM((GROUP, 16, 384), BF16),
+            pltpu.VMEM((GROUP, 16, 512), BF16),
+            pltpu.VMEM((GROUP, 16, 512), BF16),
             pltpu.VMEM((REQ, 2304, 256), BF16),
             pltpu.VMEM((1040, 256), F32),
             pltpu.VMEM((1040, 256), F32),
@@ -628,9 +684,10 @@
             pltpu.VMEM((REQ, 2, 8, 128), F32),
             pltpu.VMEM((1024, 512), BF16),
             pltpu.SMEM((REP,), jnp.int32),
-            dma((2,)), dma((3,)), dma((3, XN)), dma((3, XN)),
+            dma((2,)), dma((4,)), dma((4, XN)), dma((4, XN)),
             dma((8,)), dma((8,)), dma((2,)), dma((REP,)), dma((REP,)),
-            dma((2, 2, 4)), dma((2, 2, 4)), dma((2,)), dma((GROUP,)), dma((GROUP,)),
+            dma((2, 2, 4)), dma((2, 2, 4)), dma((2,)), dma((2, GROUP)), dma((2, GROUP)),
+            pltpu.SemaphoreType.REGULAR, pltpu.SemaphoreType.REGULAR,
         ],
         compiler_params=pltpu.CompilerParams(
             collective_id=0, has_side_effects=True, vmem_limit_bytes=60 * 2**20

time: 61 us -> 56.7 us (0.930); the launches traced: 60.8 us -> 55.8 us
  Pallas kernels: 59.2 us -> 54.2 us
    pallas_call x1, Pallas kernels: 59.2 us -> 54.2 us  [on_device(): pl.pallas_call(kernel, out_shape=jax.ShapeDtypeStruct((REQ, STEPS, HEADS...]
where the time goes in v3:
time: 56.7 us; the launch traced here: 55.8 us
  Pallas kernels  54.2 us (96%)
  local copies, waits for them, and re-layouts  1.55 us (3%)
    pallas_call x1, Pallas kernels, on_device(): pl.pallas_call(kernel, out_shape=jax.ShapeDtypeStruct((REQ, STEPS, HEADS...  54.2 us
    unnamed x1, local copies, waits for them, and re-layouts  1.55 us

profile of v3, /device:TPU:1, one launch (start us, length us, event | category | flops | bytes accessed | tf_op | source)
XLA Modules:
  0.0 55.8 jit_solution(16768363830793300627)
XLA Ops:
  0.0 54.2 %latent_attention.1 = bf16[5,4,2048]{2,1,0:T(4,128)(2,1)} custom-call(bf16[5,4,1536]{2,1,0:T(4,128)(2,1)} %bitcast.4, bf16[5,4,576]{2,1,0:T(4,128)(2,1)} %bitcast.5, bf16[320,64,512]{2,1,0:T(8,128)(2,1)} %lat_hbm.1, bf16[320,4096]{1,0:T(8,128)(2,1)} %rope_hbm.1, s32[5,64]{1,0:T(8,128)} %bt.1, s32[5]{0:T(128)} %ln.1, s32[32]{0:T(128)} %own.1, ...), custom_call_target="tpu_custom_call" | custom-call | tf_op jit(solution)/shard_map/latent_attention/pallas_call | solution.py:650
  54.2 1.6 %copy.13 = bf16[4,5,2048]{2,0,1:T(4,128)(2,1)} copy(bf16[4,5,2048]{2,0,1:T(4,128)(2,1)} %bitcast.3) | data formatting | bytes 163840

commit v4 on v3

--- a/solution.py
+++ b/solution.py
@@ -21,6 +21,7 @@
 XN = 4
 TAIL = QR // 4
 XW = QR + TAIL
+XCUT = 768
 MSG = 96
 SCALE = float((DN + DR) ** -0.5 * np.log2(np.e))
 NEG = -1e30
@@ -37,7 +38,7 @@
 
 def kernel(
     x_ref, ne_ref, lat_hbm, rope_hbm, bt, ln, own, wq_hbm, wk_hbm, wv_hbm, freq_ref, out_ref,
-    pool, zpool, rope, wx, kx, vx, wf, kf, msend, mrecv, vfull, xs, xsend, xrecv, xexp, wall,
+    pool, zpool, rope, wx, kx, vx, wf, kf, msend, mrecv, vfull, xs, xrecv, xexp, wall,
     qsend, qrecv, qsend2, qrecv2, wqt, s_a, s_b, m_sc, l_sc, acc, att, nef, cs, pick, inv,
     sem_local, sem_own, a_send, a_recv, x_send, x_recv, xc_sem, m_send, m_recv,
     v_send, v_recv, vc_sem, q_send, q_recv, row_sem, plane_sem,
@@ -123,8 +124,48 @@
     row = x_ref[4].astype(F32)
     for j in range(4):
         xs[4 * j : 4 * j + 4, QR:] = row[:, TAIL * j : TAIL * (j + 1)]
-    xsend[...] = xs[...].astype(BF16)
-
+
+    zl = lax.rem(zc, 2)
+
+    def x_cols(side):
+        return slice(0, XCUT) if side == 0 else slice(XCUT, XW)
+
+    def x_block(hop, side, zz, yy):
+        if hop == 0:
+            return xrecv.at[zz, yy, core, :, x_cols(side)]
+        if side == 0:
+            return xrecv.at[:, yy, core, :, x_cols(side)]
+        return xrecv.at[zz, :, core, :, x_cols(side)]
+
+    def x_move(hop, side, k, receive):
+        zz, yy = zl, yc
+        if (side == 0) == (hop == 0):
+            zz = 1 - zl
+            slot = 0
+        else:
+            yy = lax.rem(yc + k, 4)
+            slot = yy if receive else yc
+        block = x_block(hop, side, zz, yy) if receive else x_block(hop, side, zl, yc)
+        return pltpu.make_async_remote_copy(
+            src_ref=block, dst_ref=block, send_sem=x_send.at[hop, side, k], recv_sem=x_recv.at[hop, side, slot],
+            device_id={"rep": (zc - zl + zz) * 8 + yy * 2 + core}, device_id_type=MESH,
+        )
+
+    def x_peers(hop, side):
+        return (1,) if (side == 0) == (hop == 0) else (2, 1, 3)
+
+    def x_all(hop, act):
+        for side in (1, 0):
+            for k in x_peers(hop, side):
+                if act == "start":
+                    x_move(hop, side, k, False).start()
+                elif act == "wait":
+                    x_move(hop, side, k, True).wait_recv()
+                else:
+                    x_move(hop, side, k, False).wait_send()
+
+    xrecv[zl, yc, core] = xs[...].astype(BF16)
+    x_all(0, "start")
     pl.semaphore_wait(row_sem, 3)
     for k in range(1, 4):
         pl.semaphore_signal(plane_sem, inc=1, device_id=along("z", k), device_id_type=MESH)
@@ -138,21 +179,8 @@
 
     lax.fori_loop(0, REP, invert, 0)
 
-    pl.semaphore_wait(plane_sem, 3)
-
-    def x_copy(k):
-        to = lax.rem(cell + k, 8)
-        return pltpu.make_async_remote_copy(
-            src_ref=xsend, dst_ref=xrecv.at[cell, core], send_sem=x_send.at[k], recv_sem=x_recv.at[cell],
-            device_id={"rep": base + 2 * to + core}, device_id_type=MESH,
-        )
-
-    def x_start(k, _):
-        x_copy(k).start()
-        return 0
-
-    lax.fori_loop(1, 8, x_start, 0)
-    xrecv[cell, core] = xsend[...]
+    x_all(0, "wait")
+    x_all(1, "start")
 
     lane8 = iota((8, 128), 1)
     sub8 = iota((8, 128), 0)
@@ -174,12 +202,13 @@
         return 0
 
     lax.fori_loop(0, REQ * 9, clear, 0)
-    prow = iota((1024, 512), 0)
-    pcol = iota((1024, 512), 1)
+    prow = iota((512, 256), 0)
+    pcol = iota((512, 256), 1)
     pick[...] = jnp.where(
-        (pcol // 16 == lax.rem(prow, 64) // 2) & (lax.rem(pcol, 16) == prow // 64), 1.0, 0.0
+        (pcol // 16 == lax.rem(prow, 32) // 2) & (lax.rem(pcol, 16) == prow // 32), 1.0, 0.0
     ).astype(BF16)
 
+    pl.semaphore_wait(plane_sem, 3)
     a_wait(0)
     for k in range(XN):
         kf[4 * k : 4 * k + 4, :] = kx[k].astype(F32)
@@ -189,7 +218,7 @@
     def m_copy(h, half):
         to = half * GROUP + lax.rem(h, 8) * 2 + h // 8
         return to, pltpu.make_async_remote_copy(
-            src_ref=msend.at[h], dst_ref=mrecv.at[r], send_sem=m_send.at[to], recv_sem=m_recv.at[r],
+            src_ref=msend.at[h], dst_ref=mrecv.at[r], send_sem=m_send.at[0], recv_sem=m_recv.at[0],
             device_id={"rep": to}, device_id_type=MESH,
         )
 
@@ -234,17 +263,9 @@
     a_start(3)
     mrecv[r] = msend[head]
 
-    def x_wait(k, _):
-        frm = lax.rem(cell + k, 8)
-        pltpu.make_async_remote_copy(
-            src_ref=xsend, dst_ref=xrecv.at[frm, core], send_sem=x_send.at[k], recv_sem=x_recv.at[frm],
-            device_id={"rep": base + 2 * frm + core}, device_id_type=MESH,
-        ).wait_recv()
-        return 0
-
-    lax.fori_loop(1, 8, x_wait, 0)
+    x_all(1, "wait")
     xc = pltpu.make_async_remote_copy(
-        src_ref=xrecv.at[:, core], dst_ref=xrecv.at[:, core], send_sem=xc_sem.at[0], recv_sem=xc_sem.at[1],
+        src_ref=xrecv.at[:, :, core], dst_ref=xrecv.at[:, :, core], send_sem=xc_sem.at[0], recv_sem=xc_sem.at[1],
         device_id={"rep": other}, device_id_type=MESH,
     )
     xc.start()
@@ -301,70 +322,80 @@
             for k in (1, 3, 2):
                 v_wait(hop, side, k)
 
-    v_start(0)
-
     rope_copy.wait()
 
     def rope_step(a, _):
         top = pl.multiple_of(a * 32, 32)
-        cat = jnp.concatenate(
-            [
-                jnp.concatenate(
-                    [rope[pl.ds(top, 16), 128 * j : 128 * j + 128], rope[pl.ds(top + 16, 16), 128 * j : 128 * j + 128]],
-                    axis=1,
-                )
-                for j in range(32)
-            ],
-            axis=0,
-        )
-        keep = (iota((256, 128), 1) < DR) == (lax.rem(iota((256, 128), 0), 2) == 0)
-        for b in range(4):
-            got = jnp.dot(pick[256 * b : 256 * b + 256, :], cat, preferred_element_type=F32)
+        keep = (iota((512, 128), 1) < DR) == (lax.rem(iota((512, 128), 0), 2) == 0)
+        for b in range(2):
+            cat = jnp.concatenate(
+                [
+                    jnp.concatenate(
+                        [
+                            rope[pl.ds(top, 16), 128 * j : 128 * j + 128],
+                            rope[pl.ds(top + 16, 16), 128 * j : 128 * j + 128],
+                        ],
+                        axis=1,
+                    )
+                    for j in range(16 * b, 16 * b + 16)
+                ],
+                axis=0,
+            )
+            got = jnp.dot(pick[...], cat, preferred_element_type=F32)
             for g in range(2):
                 v = got[:, 128 * g : 128 * g + 128]
                 v = jnp.where(keep, v, pltpu.roll(v, DR, 1)).astype(BF16)
-                zpool[pl.ds(a * 32 + g * 16 + b * 4, 4)] = v.reshape(4, 64, 128)
+                zpool[pl.ds(a * 32 + g * 16, 16), 32 * b : 32 * b + 32] = v.reshape(16, 32, 128)
         return 0
 
     lax.fori_loop(0, POOL // 32, rope_step, 0)
 
     pltpu.make_async_remote_copy(
-        src_ref=xrecv.at[:, 1 - core], dst_ref=xrecv.at[:, 1 - core], send_sem=xc_sem.at[0], recv_sem=xc_sem.at[1],
+        src_ref=xrecv.at[:, :, 1 - core], dst_ref=xrecv.at[:, :, 1 - core], send_sem=xc_sem.at[0], recv_sem=xc_sem.at[1],
         device_id={"rep": other}, device_id_type=MESH,
     ).wait_recv()
 
+    masks = [jnp.where(iota((16, TAIL), 0) // 4 == j, 1.0, 0.0).astype(BF16) for j in range(4)]
+
     def spread(n, _):
-        got = xrecv[n // 2, lax.rem(n, 2)]
-        xexp[n, 0:16, :] = got[:, :QR]
-        for j in range(4):
-            mask = jnp.where(iota((16, TAIL), 0) // 4 == j, 1.0, 0.0).astype(BF16)
-            xexp[n, 16:32, TAIL * j : TAIL * (j + 1)] = got[:, QR:] * mask
+        for d in range(4):
+            got = xrecv[n // 2, 2 * lax.rem(n, 2) + d // 2, d % 2]
+            xexp[4 * n + d, 0:16, :] = got[:, :QR]
+            for j in range(4):
+                xexp[4 * n + d, 16:32, TAIL * j : TAIL * (j + 1)] = got[:, QR:] * masks[j]
         return 0
 
-    lax.fori_loop(0, GROUP, spread, 0)
-
-    def m_wait(k, _):
-        frm = lax.rem(r + k, REP)
-        pltpu.make_async_remote_copy(
-            src_ref=mrecv.at[frm], dst_ref=mrecv.at[frm], send_sem=m_send.at[k], recv_sem=m_recv.at[frm],
-            device_id={"rep": frm}, device_id_type=MESH,
-        ).wait_recv()
+    lax.fori_loop(0, GROUP // 4, spread, 0)
+
+    def m_wait():
+        block = mrecv.at[0 : REP - 1]
+        return pltpu.make_async_remote_copy(
+            src_ref=block, dst_ref=block, send_sem=m_send.at[0], recv_sem=m_recv.at[0],
+            device_id={"rep": other}, device_id_type=MESH,
+        )
+
+    for n in range(4):
+        for k in range(1, XN):
+            a_copy(n, k).wait_send()
+    x_all(0, "drain")
+    x_all(1, "drain")
+    m_wait().wait_recv()
+    v_start(0)
+
+    def place(n, _):
+        low = iota((24, 128), 1) < DR
+        for d in range(8):
+            j = n * 8 + d
+            block = mrecv[inv[j]]
+            rows = pl.ds(pl.multiple_of(j * 48, 16), 48)
+            wall[rows, 0:128] = block[0:48]
+            t = block[64:96].astype(F32)[:24]
+            t_r = pltpu.roll(t, DR, 1)
+            both = jnp.concatenate([jnp.where(low, t, t_r), jnp.where(low, t_r, t)], axis=0)
+            wall[rows, 128:256] = both.astype(BF16)
         return 0
 
-    lax.fori_loop(1, REP, m_wait, 0)
-
-    def place(j, _):
-        block = mrecv[inv[j]]
-        rows = pl.ds(pl.multiple_of(j * 48, 16), 48)
-        wall[rows, 0:128] = block[0:48]
-        t = block[64:96].astype(F32)[:24]
-        t_r = pltpu.roll(t, DR, 1)
-        low = iota((24, 128), 1) < DR
-        both = jnp.concatenate([jnp.where(low, t, t_r), jnp.where(low, t_r, t)], axis=0)
-        wall[rows, 128:256] = both.astype(BF16)
-        return 0
-
-    lax.fori_loop(0, REP, place, 0)
+    lax.fori_loop(0, REP // 8, place, 0)
 
     key = mrecv[:, 48:64, :].reshape(LAT, 128)
     key = jnp.concatenate([key, key], axis=1)
@@ -375,7 +406,7 @@
     def q_copy(n, to):
         src, dst = qparts[n]
         return pltpu.make_async_remote_copy(
-            src_ref=src.at[to], dst_ref=dst.at[head], send_sem=q_send.at[n, to], recv_sem=q_recv.at[n, mine],
+            src_ref=src.at[to], dst_ref=dst.at[head], send_sem=q_send.at[n], recv_sem=q_recv.at[n],
             device_id={"rep": base + to}, device_id_type=MESH,
         )
 
@@ -427,26 +458,18 @@
     qrecv[head] = qsend[mine]
     qrecv2[head] = qsend2[mine]
 
-    v_wait_all(0)
-    v_start(1)
-
+    xc.wait_send()
+    m_wait().wait_send()
     perm_row = iota((256, 256), 0)
     want = lax.rem(perm_row // 4, 16) * 16 + (perm_row // 64) * 4 + lax.rem(perm_row, 4)
     perm = jnp.where(iota((256, 256), 1) == want, 1.0, 0.0).astype(BF16)
 
-    def q_wait_all(n):
-        src, dst = qparts[n]
-
-        def q_wait(k, _):
-            frm = lax.rem(mine + k, GROUP)
-            slot = lax.rem(frm, 2) * 8 + frm // 2
-            pltpu.make_async_remote_copy(
-                src_ref=src.at[frm], dst_ref=dst.at[slot], send_sem=q_send.at[n, frm], recv_sem=q_recv.at[n, frm],
-                device_id={"rep": base + frm}, device_id_type=MESH,
-            ).wait_recv()
-            return 0
-
-        lax.fori_loop(1, GROUP, q_wait, 0)
+    def q_wait(n):
+        block = qparts[n][1].at[0 : GROUP - 1]
+        return pltpu.make_async_remote_copy(
+            src_ref=block, dst_ref=block, send_sem=q_send.at[n], recv_sem=q_recv.at[n],
+            device_id={"rep": other}, device_id_type=MESH,
+        )
 
     low_q = iota((LAT, 128), 1) < DR
     low_r = iota((DR, 128), 1) < DR
@@ -472,7 +495,7 @@
         wqt[i, 2240:2304, 128:256] = rright
 
     def queries(n):
-        q_wait_all(n)
+        q_wait(n).wait_recv()
         dst = qparts[n][1]
         got = jnp.dot(perm, dst[...].reshape(GROUP * 16, dst.shape[2]), preferred_element_type=F32)
         for m in range(2):
@@ -484,6 +507,8 @@
             stationary(4, lat_i, got[128:192, 256:384])
 
     queries(0)
+    v_wait_all(0)
+    v_start(1)
     pool_copy.wait()
 
     def page(i, c, k, g):
@@ -592,6 +617,9 @@
             finish(i - 1)
         if i == 3:
             forward()
+
+    q_wait(0).wait_send()
+    q_wait(1).wait_send()
 
     pltpu.make_async_remote_copy(
         src_ref=vfull.at[:, :, 1 - core], dst_ref=vfull.at[:, :, 1 - core], send_sem=vc_sem.at[0], recv_sem=vc_sem.at[1],
@@ -605,30 +633,6 @@
             out_ref[i, :, 256 * p : 256 * p + 128] = o[i, 0:4, 0:128].astype(BF16)
             out_ref[i, :, 256 * p + 128 : 256 * p + 256] = o[i, 4:8, 128:256].astype(BF16)
 
-    for n in range(4):
-        for k in range(1, XN):
-            a_copy(n, k).wait_send()
-
-    def drain(k, _):
-        x_copy(k).wait_send()
-        return 0
-
-    lax.fori_loop(1, 8, drain, 0)
-    xc.wait_send()
-
-    def drain_m(k, _):
-        to = lax.rem(r + k, REP)
-        m_copy(lax.rem(to, GROUP) // 2 + 8 * lax.rem(to, 2), to // GROUP)[1].wait_send()
-        return 0
-
-    lax.fori_loop(1, REP, drain_m, 0)
-
-    def drain_q(k, _):
-        q_copy(0, lax.rem(mine + k, GROUP)).wait_send()
-        q_copy(1, lax.rem(mine + k, GROUP)).wait_send()
-        return 0
-
-    lax.fori_loop(1, GROUP, drain_q, 0)
     for hop in range(2):
         for side in range(2):
             for k in range(1, 4):
@@ -665,8 +669,7 @@
             pltpu.VMEM((REP, MSG, 128), BF16),
             pltpu.VMEM((4, 4, 2, 16, 2048), BF16),
             pltpu.VMEM((16, XW), F32),
-            pltpu.VMEM((16, XW), BF16),
-            pltpu.VMEM((8, 2, 16, XW), BF16),
+            pltpu.VMEM((2, 4, 2, 16, XW), BF16),
             pltpu.VMEM((GROUP, 32, QR), BF16),
             pltpu.VMEM((QR, 256), BF16),
             pltpu.VMEM((GROUP, 16, 384), BF16),
@@ -682,11 +685,11 @@
             pltpu.VMEM((REQ, 64, LAT), F32),
             pltpu.VMEM((REQ, 8, 640), F32),
             pltpu.VMEM((REQ, 2, 8, 128), F32),
-            pltpu.VMEM((1024, 512), BF16),
+            pltpu.VMEM((512, 256), BF16),
             pltpu.SMEM((REP,), jnp.int32),
             dma((2,)), dma((4,)), dma((4, XN)), dma((4, XN)),
-            dma((8,)), dma((8,)), dma((2,)), dma((REP,)), dma((REP,)),
-            dma((2, 2, 4)), dma((2, 2, 4)), dma((2,)), dma((2, GROUP)), dma((2, GROUP)),
+            dma((2, 2, 4)), dma((2, 2, 4)), dma((2,)), dma((1,)), dma((1,)),
+            dma((2, 2, 4)), dma((2, 2, 4)), dma((2,)), dma((2,)), dma((2,)),
             pltpu.SemaphoreType.REGULAR, pltpu.SemaphoreType.REGULAR,
         ],
         compiler_params=pltpu.CompilerParams(

time: 56.7 us -> 48.2 us (0.85); the launches traced: 55.8 us -> 48 us
  Pallas kernels: 54.2 us -> 46.5 us
    pallas_call x1, Pallas kernels: 54.2 us -> 46.5 us  [on_device(): pl.pallas_call(kernel, out_shape=jax.ShapeDtypeStruct((REQ, STEPS, HEADS...]
where the time goes in v4:
time: 48.2 us; the launch traced here: 48 us
  Pallas kernels  46.5 us (96%)
  local copies, waits for them, and re-layouts  1.55 us (3%)
    pallas_call x1, Pallas kernels, on_device(): pl.pallas_call(kernel, out_shape=jax.ShapeDtypeStruct((REQ, STEPS, HEADS...  46.5 us
    unnamed x1, local copies, waits for them, and re-layouts  1.55 us

profile of v4, /device:TPU:1, one launch (start us, length us, event | category | flops | bytes accessed | tf_op | source)
XLA Modules:
  0.0 48.0 jit_solution(10741860663043058655)
XLA Ops:
  0.0 46.5 %latent_attention.1 = bf16[5,4,2048]{2,1,0:T(4,128)(2,1)} custom-call(bf16[5,4,1536]{2,1,0:T(4,128)(2,1)} %bitcast.4, bf16[5,4,576]{2,1,0:T(4,128)(2,1)} %bitcast.5, bf16[320,64,512]{2,1,0:T(8,128)(2,1)} %lat_hbm.1, bf16[320,4096]{1,0:T(8,128)(2,1)} %rope_hbm.1, s32[5,64]{1,0:T(8,128)} %bt.1, s32[5]{0:T(128)} %ln.1, s32[32]{0:T(128)} %own.1, ...), custom_call_target="tpu_custom_call" | custom-call | tf_op jit(solution)/shard_map/latent_attention/pallas_call | solution.py:654
  46.5 1.6 %copy.13 = bf16[4,5,2048]{2,0,1:T(4,128)(2,1)} copy(bf16[4,5,2048]{2,0,1:T(4,128)(2,1)} %bitcast.3) | data formatting | bytes 163840

commit v5 on v4

--- a/solution.py
+++ b/solution.py
@@ -22,7 +22,7 @@
 TAIL = QR // 4
 XW = QR + TAIL
 XCUT = 768
-MSG = 96
+MSG = 88
 SCALE = float((DN + DR) ** -0.5 * np.log2(np.e))
 NEG = -1e30
 GATHER = 2
@@ -230,15 +230,14 @@
         last = wf[:, pl.ds(pl.multiple_of(col + 256, 128), 128)]
         mid_r = pltpu.roll(mid, DR, 1)
         last_r = pltpu.roll(last, DR, 1)
-        pad = jnp.zeros((8, 128), F32)
-        even = jnp.concatenate([jnp.where(low24, mid[:24], mid_r[24:]), pad], axis=0)
-        odd = jnp.concatenate([jnp.where(low24, last_r[:24], last[24:]), pad], axis=0)
+        even = jnp.where(low24, mid[:24], mid_r[24:])
+        odd = jnp.where(low24, last_r[:24], last[24:])
         msend[2 * p, 0:48] = first.astype(BF16)
         msend[2 * p, 48:64] = kf[:, pl.ds(pl.multiple_of(p * 256, 128), 128)].astype(BF16)
-        msend[2 * p, 64:96] = even.astype(BF16)
+        msend[2 * p, 64:88] = even.astype(BF16)
         msend[2 * p + 1, 0:48] = jnp.where(low48, mid_r, last_r).astype(BF16)
         msend[2 * p + 1, 48:64] = kf[:, pl.ds(pl.multiple_of(p * 256 + 128, 128), 128)].astype(BF16)
-        msend[2 * p + 1, 64:96] = odd.astype(BF16)
+        msend[2 * p + 1, 64:88] = odd.astype(BF16)
         for half in range(2):
             for g in range(2):
                 to, copy = m_copy(2 * p + g, half)
@@ -389,7 +388,7 @@
             block = mrecv[inv[j]]
             rows = pl.ds(pl.multiple_of(j * 48, 16), 48)
             wall[rows, 0:128] = block[0:48]
-            t = block[64:96].astype(F32)[:24]
+            t = block[64:88].astype(F32)
             t_r = pltpu.roll(t, DR, 1)
             both = jnp.concatenate([jnp.where(low, t, t_r), jnp.where(low, t_r, t)], axis=0)
             wall[rows, 128:256] = both.astype(BF16)
@@ -620,6 +619,10 @@
 
     q_wait(0).wait_send()
     q_wait(1).wait_send()
+    for hop in range(2):
+        for side in range(2):
+            for k in range(1, 4):
+                v_copy(hop, side, k).wait_send()
 
     pltpu.make_async_remote_copy(
         src_ref=vfull.at[:, :, 1 - core], dst_ref=vfull.at[:, :, 1 - core], send_sem=vc_sem.at[0], recv_sem=vc_sem.at[1],
@@ -633,10 +636,6 @@
             out_ref[i, :, 256 * p : 256 * p + 128] = o[i, 0:4, 0:128].astype(BF16)
             out_ref[i, :, 256 * p + 128 : 256 * p + 256] = o[i, 4:8, 128:256].astype(BF16)
 
-    for hop in range(2):
-        for side in range(2):
-            for k in range(1, 4):
-                v_copy(hop, side, k).wait_send()
     pltpu.make_async_remote_copy(
         src_ref=vfull.at[:, :, core], dst_ref=vfull.at[:, :, core], send_sem=vc_sem.at[0], recv_sem=vc_sem.at[1],
         device_id={"rep": other}, device_id_type=MESH,

time: 48.2 us -> 47.5 us (0.985)
  Pallas kernels: 46.5 us -> 45.7 us
    pallas_call x1, Pallas kernels: 46.5 us -> 45.7 us  [on_device(): pl.pallas_call(kernel, out_shape=jax.ShapeDtypeStruct((REQ, STEPS, HEADS...]
where the time goes in v5:
time: 47.5 us; the launch traced here: 47.3 us
  Pallas kernels  45.7 us (96%)
  local copies, waits for them, and re-layouts  1.55 us (3%)
    pallas_call x1, Pallas kernels, on_device(): pl.pallas_call(kernel, out_shape=jax.ShapeDtypeStruct((REQ, STEPS, HEADS...  45.7 us
    unnamed x1, local copies, waits for them, and re-layouts  1.55 us

profile of v5, /device:TPU:1, one launch (start us, length us, event | category | flops | bytes accessed | tf_op | source)
XLA Modules:
  0.0 47.3 jit_solution(16645424388637508260)
XLA Ops:
  0.0 45.7 %latent_attention.1 = bf16[5,4,2048]{2,1,0:T(4,128)(2,1)} custom-call(bf16[5,4,1536]{2,1,0:T(4,128)(2,1)} %bitcast.4, bf16[5,4,576]{2,1,0:T(4,128)(2,1)} %bitcast.5, bf16[320,64,512]{2,1,0:T(8,128)(2,1)} %lat_hbm.1, bf16[320,4096]{1,0:T(8,128)(2,1)} %rope_hbm.1, s32[5,64]{1,0:T(8,128)} %bt.1, s32[5]{0:T(128)} %ln.1, s32[32]{0:T(128)} %own.1, ...), custom_call_target="tpu_custom_call" | custom-call | tf_op jit(solution)/shard_map/latent_attention/pallas_call | solution.py:653
  45.7 1.6 %copy.13 = bf16[4,5,2048]{2,0,1:T(4,128)(2,1)} copy(bf16[4,5,2048]{2,0,1:T(4,128)(2,1)} %bitcast.3) | data formatting | bytes 163840

commit v6 on v5

--- a/solution.py
+++ b/solution.py
@@ -497,15 +497,21 @@
         q_wait(n).wait_recv()
         dst = qparts[n][1]
         got = jnp.dot(perm, dst[...].reshape(GROUP * 16, dst.shape[2]), preferred_element_type=F32)
-        for m in range(2):
-            left = got[64 * m : 64 * m + 64, :256]
-            right = got[128 + 64 * m : 192 + 64 * m, :256]
-            stationary(2 * n + m, jnp.concatenate([left, right], axis=1), got[64 * m : 64 * m + 64, 256:384])
-        if n == 1:
-            lat_i = jnp.concatenate([got[64 * j : 64 * j + 64, 384:512] for j in range(4)], axis=1)
-            stationary(4, lat_i, got[128:192, 256:384])
-
-    queries(0)
+
+        def build(i):
+            m = i - 2 * n
+            if m < 2:
+                left = got[64 * m : 64 * m + 64, :256]
+                right = got[128 + 64 * m : 192 + 64 * m, :256]
+                stationary(i, jnp.concatenate([left, right], axis=1), got[64 * m : 64 * m + 64, 256:384])
+            else:
+                lat_i = jnp.concatenate([got[64 * j : 64 * j + 64, 384:512] for j in range(4)], axis=1)
+                stationary(i, lat_i, got[128:192, 256:384])
+
+        return build
+
+    build = queries(0)
+    build(0)
     v_wait_all(0)
     v_start(1)
     pool_copy.wait()
@@ -599,7 +605,9 @@
     bufs = (s_a, s_b)
     for i in range(REQ + 1):
         if i == 2:
-            queries(1)
+            build = queries(1)
+        if 0 < i < REQ:
+            build(i)
         if i < REQ:
             fresh(i, bufs[i % 2], i % 2)
         if i > 0:

time: 47.5 us -> 47.5 us (level)
  no operation moved by 1% of the time
where the time goes in v6:
time: 47.5 us; the launch traced here: 47.3 us
  Pallas kernels  45.7 us (96%)
  local copies, waits for them, and re-layouts  1.55 us (3%)
    pallas_call x1, Pallas kernels, on_device(): pl.pallas_call(kernel, out_shape=jax.ShapeDtypeStruct((REQ, STEPS, HEADS...  45.7 us
    unnamed x1, local copies, waits for them, and re-layouts  1.55 us

profile of v6, /device:TPU:1, one launch (start us, length us, event | category | flops | bytes accessed | tf_op | source)
XLA Modules:
  0.0 47.3 jit_solution(7137177432031538192)
XLA Ops:
  0.0 45.7 %latent_attention.1 = bf16[5,4,2048]{2,1,0:T(4,128)(2,1)} custom-call(bf16[5,4,1536]{2,1,0:T(4,128)(2,1)} %bitcast.4, bf16[5,4,576]{2,1,0:T(4,128)(2,1)} %bitcast.5, bf16[320,64,512]{2,1,0:T(8,128)(2,1)} %lat_hbm.1, bf16[320,4096]{1,0:T(8,128)(2,1)} %rope_hbm.1, s32[5,64]{1,0:T(8,128)} %bt.1, s32[5]{0:T(128)} %ln.1, s32[32]{0:T(128)} %own.1, ...), custom_call_target="tpu_custom_call" | custom-call | tf_op jit(solution)/shard_map/latent_attention/pallas_call | solution.py:661
  45.7 1.6 %copy.13 = bf16[4,5,2048]{2,0,1:T(4,128)(2,1)} copy(bf16[4,5,2048]{2,0,1:T(4,128)(2,1)} %bitcast.3) | data formatting | bytes 163840
